TPU v7x, 256 devices: a whole 4x4x8 slice. The times are simulated.
256 devices in a mesh: freq: 16 (over y, x), rows: 16 (over z, core).
Axes of the slice: x: 4, y: 4, z: 8, core: 2. Of those that a mesh axis runs over, the one named last changes fastest.
Arguments:
- basis: float32 [64, 64, 2, 128, 256], P('freq', 'rows'), parts along dimension 0, may hold values from -40 to 40
- near_blocks: bfloat16 [512, 32, 128, 128], P('rows', 'freq'), parts along dimension 1, may hold values from -0.125 to 0.125
- near_pairs: int32 [512, 2], P('rows'), may hold values from 0 to 63, as said below
- bfly_weights: bfloat16 [96, 64, 4, 128, 128], P('freq', 'rows'), parts along dimension 0, may hold values from -0.25 to 0.25
- partner_local: int32 [6, 64], P(None, 'rows'), may hold values from 0 to 3
Outputs:
- next_vector: float32 [64, 32, 128, 256], P('rows', 'freq'), parts along dimension 1
- coeffs: float32 [80, 2, 256], P('freq'), parts along dimension 0
There are 16 independent parts, one for each index of `freq`. A program takes and returns all parts, laid end to end along the dimension named above; an argument that names none is the same for every part. Nothing has to cross between parts.
Inputs may be any that keep to these rules, and one draw needn't show every extreme that they name: `near_pairs`: the first 28 slots of each device hold blocks of that device's own block rows; the other 4 hold blocks shipped to it, of any block row. A slot's column block lies within 2 blocks of its row block.
All inputs are finite; a program needn't handle non-finite values.
Results may differ from a plain program's by a relative error of at most 0.0065.
Values may be sent and summed in bfloat16 or wider, within the bound.
No kernel may reach another device: no remote copies, remote signals or barrier semaphores. Data moves between devices by JAX's collectives and lax.ppermute only.
A program may use at most 192 MiB of HBM per device.

v0:
```python
import jax
import jax.numpy as jnp
from jax import lax
from jax.sharding import PartitionSpec as P

LEVELS = 6


def swapped(value, axis, stride):
    mask = 2**stride
    pairs = [(source, source ^ mask) for source in range(lax.axis_size(axis))]
    return lax.ppermute(value, axis, pairs)


def complex_blocks(blocks, vectors):

    def single(left, right):
        return jnp.einsum("sij,sjr->sir", left, right, preferred_element_type=jnp.float32)

    real = single(blocks[:, 0], vectors[:, 0]) - single(blocks[:, 1], vectors[:, 1])
    imag = single(blocks[:, 0], vectors[:, 1]) + single(blocks[:, 1], vectors[:, 0])
    return jnp.stack([real, imag], axis=1)


def shards(basis, near_blocks, near_pairs, bfly_weights, partner_local):
    blocks_here = basis.shape[1]
    entries = basis.shape[3]
    total_blocks = blocks_here * lax.axis_size("rows")
    last = basis[-1]
    xv = last.astype(jnp.bfloat16)
    whole = lax.all_gather(xv, "rows", axis=0, tiled=True)
    prods = complex_blocks(near_blocks, whole[near_pairs[:, 1]])
    rows_of = near_pairs[:, 0]
    wanted = lax.iota(jnp.int32, lax.axis_size("rows") * blocks_here)
    onehot = (wanted[:, None] == rows_of[None, :]).astype(jnp.float32)
    near = lax.psum_scatter(
        jnp.einsum("bs,sxyz->bxyz", onehot, prods, precision=lax.Precision.HIGHEST).astype(
            jnp.bfloat16
        ),
        "rows",
        scatter_dimension=0,
        tiled=True,
    ).astype(jnp.float32)
    local_levels = blocks_here.bit_length() - 1
    section = xv
    for level in range(LEVELS):
        if level < local_levels:
            source = section
        else:
            source = swapped(section, "rows", level - local_levels)
        picked = source[partner_local[level]]
        weights = bfly_weights[level]
        section = (
            complex_blocks(weights[:, 0:2], section) + complex_blocks(weights[:, 2:4], picked)
        ).astype(jnp.bfloat16)
    product = last + near + section.astype(jnp.float32)
    scale = 1.0 / (total_blocks * entries)
    basis_re = basis[:, :, 0]
    basis_im = basis[:, :, 1]
    prod_re = product[:, 0]
    prod_im = product[:, 1]
    highest = lax.Precision.HIGHEST
    local_re = (
        jnp.einsum("knbr,nbr->kr", basis_re, prod_re, precision=highest)
        + jnp.einsum("knbr,nbr->kr", basis_im, prod_im, precision=highest)
    ) * scale
    local_im = (
        jnp.einsum("knbr,nbr->kr", basis_re, prod_im, precision=highest)
        - jnp.einsum("knbr,nbr->kr", basis_im, prod_re, precision=highest)
    ) * scale
    proj_re, proj_im = lax.psum((local_re, local_im), "rows")
    orth_re = prod_re - jnp.sum(
        basis_re * proj_re[:, None, None, :] - basis_im * proj_im[:, None, None, :], axis=0
    )
    orth_im = prod_im - jnp.sum(
        basis_re * proj_im[:, None, None, :] + basis_im * proj_re[:, None, None, :], axis=0
    )
    local_orth = jnp.sum(orth_re * orth_re + orth_im * orth_im, axis=(0, 1)) * scale
    mean_square = lax.psum(local_orth, "rows")
    norm_value = jnp.sqrt(mean_square + 1e-06)
    next_vector = jnp.stack([orth_re, orth_im], axis=1) / norm_value
    head = jnp.stack([proj_re, proj_im], axis=1)
    tail = jnp.stack([norm_value, jnp.zeros_like(norm_value)], axis=0)[None]
    coeffs = jnp.concatenate([head, tail], axis=0)
    return (next_vector, coeffs)


def solution(mesh):
    placed = (
        P("freq", "rows", None, None, None),
        P("rows", "freq", None, None),
        P("rows", None),
        P("freq", "rows", None, None, None),
        P(None, "rows"),
    )
    return jax.shard_map(
        shards,
        mesh=mesh,
        in_specs=placed,
        out_specs=(P("rows", "freq", None, None), P("freq", None, None)),
        check_vma=False,
    )
```

profile of v0, /device:TPU:1, one launch (start us, length us, event | category | flops | bytes accessed | tf_op | source)
XLA Modules:
  0.0 293.1 jit_solution(7183252768654975194)
XLA Ops:
  7.2 1.3 fusion.44
  8.5 0.8 copy.108
  9.4 0.8 slice_bitcast_fusion.152
  10.2 60.4 %all-gather.2.cloned.1.call-done = bf16[64,2,128,256]{3,2,1,0:T(8,128)(2,1)} async-done(((bf16[4,2,128,256]{3,2,1,0:T(8,128)(2,1)}), bf16[64,2,128,256]{3,2,1,0:T(8,128)(2,1)}) %all-gather.2.cloned.1.call-update) | async-done | bytes 8388624 | tf_op jit(solution)/shard_map/all_gather | solution.py:31
  70.6 6.2 %gather_fusion = bf16[32,2,128,256]{3,2,1,0:T(8,128)(2,1)} fusion(bf16[64,2,128,256]{3,2,1,0:T(8,128)(2,1)} %all-gather.2.cloned.1.call-done, s32[1024]{0:T(1024)S(1)} %pad_clamp_fusion.6), kind=kCustom, calls=%fused_computation | custom fusion | bytes 8388736 | tf_op jit(solution)/shard_map/gather | solution.py:32
  76.7 2.5 fusion.9
  79.2 0.3 copy-done
  79.6 0.8 fusion.8
  80.3 0.8 add_bitcast_fusion
  81.2 0.8 subtract_bitcast_fusion
  82.0 3.8 %pad_maximum_fusion = f32[32,2,128,256]{2,3,0,1:T(8,128)} fusion(f32[32,1,128,256]{2,3,0,1:T(8,128)S(1)} %add_bitcast_fusion, f32[32,1,128,256]{2,3,0,1:T(8,128)S(1)} %subtract_bitcast_fusion), kind=kLoop, calls=%fused_computation.7 | loop fusion | flops 2097152 | bytes 16777216 | tf_op jit(solution)/shard_map/stack | solution.py:22
  85.8 10.3 %copy.113 = f32[32,2,128,256]{3,0,2,1:T(8,128)} copy(f32[32,2,128,256]{2,3,0,1:T(8,128)} %pad_maximum_fusion) | data formatting | bytes 16777216 | tf_op jit(solution)/shard_map/stack | solution.py:22
  96.1 11.8 %convolution_convert_fusion = bf16[64,2,128,256]{3,0,2,1:T(8,128)(2,1)} fusion(f32[32,2,128,256]{3,0,2,1:T(8,128)} %copy.113, s32[32]{0:T(128)S(1)} %get-tuple-element.34), kind=kOutput, calls=%fused_computation.8 | convolution fusion | flops 1614809088 | bytes 16777344 | tf_op jit(solution)/shard_map/bs,sxyz->bxyz/dot_general | solution.py:37
  107.9 11.4 %copy.114 = bf16[64,2,128,256]{3,2,1,0:T(8,128)(2,1)} copy(bf16[64,2,128,256]{3,0,2,1:T(8,128)(2,1)} %convolution_convert_fusion) | data formatting | bytes 16777216 | tf_op jit(solution)/shard_map/convert_element_type | solution.py:37
  119.3 0.7 copy-done.8
  120.3 0.6 gather_fusion.1
  120.9 3.1 %fusion.87 = (bf16[1,4,4,128,128]{4,3,2,1,0:T(8,128)(2,1)}, bf16[1,4,4,128,128]{4,3,2,1,0:T(8,128)(2,1)S(1)}, bf16[1,4,4,128,128]{4,3,2,1,0:T(8,128)(2,1)S(1)}, ...) fusion(bf16[6,4,4,128,128]{4,3,2,1,0:T(8,128)(2,1)} %param.8), kind=kLoop, calls=%fused_computation.227 | loop fusion | bytes 6291456 | tf_op jit(solution)/shard_map/slice | solution.py:52
  126.1 0.6 gather_fusion.2
  126.7 0.3 fusion.60
  126.9 0.3 fusion.28
  127.2 0.3 fusion.59
  127.5 0.3 fusion.29
  127.8 0.3 fusion.58
  128.1 0.3 fusion.30
  128.4 0.3 fusion.57
  128.7 0.3 fusion.31
  129.1 0.3 collective-permute-start
  129.7 1.0 fusion.26
  131.2 1.0 fusion.27
  132.2 1.7 gather_fusion.3
  135.1 0.3 collective-permute-start.1
  136.4 18.2 %collective-permute-done.1 = bf16[4,2,128,256]{2,3,0,1:T(8,128)(2,1)} collective-permute-done((bf16[4,2,128,256]{2,3,0,1:T(8,128)(2,1)S(1)}, bf16[4,2,128,256]{2,3,0,1:T(8,128)(2,1)}, u32[]{:S(2)}, u32[]{:S(2)}) %collective-permute-start.1) | collective-permute-done | bytes 524320 | tf_op jit(solution)/shard_map/ppermute | solution.py:12
  154.6 1.7 gather_fusion.4
  157.3 1.3 collective-permute-start.2
  159.6 29.2 %collective-permute-done.2 = bf16[4,2,128,256]{2,3,0,1:T(8,128)(2,1)S(1)} collective-permute-done((bf16[4,2,128,256]{2,3,0,1:T(8,128)(2,1)S(1)}, bf16[4,2,128,256]{2,3,0,1:T(8,128)(2,1)S(1)}, u32[]{:S(2)}, u32[]{:S(2)}) %collective-permute-start.2) | collective-permute-done | bytes 524320 | tf_op jit(solution)/shard_map/ppermute | solution.py:12
  188.7 0.6 gather_fusion.5
  190.4 2.6 collective-permute-start.3
  193.9 30.2 %collective-permute-done.3 = bf16[4,2,128,256]{2,3,0,1:T(8,128)(2,1)S(1)} collective-permute-done((bf16[4,2,128,256]{2,3,0,1:T(8,128)(2,1)S(1)}, bf16[4,2,128,256]{2,3,0,1:T(8,128)(2,1)S(1)}, u32[]{:S(2)}, u32[]{:S(2)}) %collective-permute-start.3) | collective-permute-done | bytes 524320 | tf_op jit(solution)/shard_map/ppermute | solution.py:12
  224.1 0.6 gather_fusion.6
  225.7 4.6 %reduce-scatter.2.cloned.1.call-done = bf16[4,2,128,256]{3,2,1,0:T(8,128)(2,1)} async-done(((bf16[64,2,128,256]{3,2,1,0:T(8,128)(2,1)}), bf16[4,2,128,256]{3,2,1,0:T(8,128)(2,1)}) %reduce-scatter.2.cloned.1.call-update) | async-done | bytes 524304 | tf_op jit(solution)/shard_map/reduce_scatter | solution.py:36
  230.4 1.8 convert_add_fusion
  232.2 0.8 copy-done.1
  233.0 0.6 fusion.6
  233.7 23.4 %all-reduce.1 = (f32[4,256]{1,0:T(4,128)S(1)}, f32[4,256]{1,0:T(4,128)S(1)}) all-reduce(f32[4,256]{1,0:T(4,128)S(1)} %multiply_bitcast_fusion, f32[4,256]{1,0:T(4,128)S(1)} %multiply_bitcast_fusion.1), channel_id=1, replica_groups=mesh['freq'=16,'rows'=16] {'rows'}, use_global_device_ids=true, to_apply=%region_2.0 | all-reduce | flops 2048 | bytes 16384 | tf_op jit(solution)/shard_map/psum | solution.py:71
  257.1 3.0 %fusion.5 = (f32[4,128,256]{2,1,0:T(8,128)S(1)}, f32[4,128,256]{2,1,0:T(8,128)S(1)}) fusion(f32[4,4,2,128,256]{4,3,2,1,0:T(8,128)} %param.5, f32[4,256]{1,0:T(4,128)S(1)} %get-tuple-element.22, f32[4,256]{1,0:T(4,128)S(1)} %get-tuple-element.23), kind=kLoop, calls=%fused_computation.22 | loop fusion | flops 3932160 | bytes 5251072 | tf_op jit(solution)/shard_map/reduce_sum | solution.py:72
  260.5 24.0 %psum.23 = f32[256]{0:T(256)S(1)} all-reduce(f32[256]{0:T(256)S(1)} %broadcast_multiply_fusion), channel_id=1, replica_groups=mesh['freq'=16,'rows'=16] {'rows'}, use_global_device_ids=true, to_apply=%region_6.0 | all-reduce | flops 256 | bytes 2048 | tf_op jit(solution)/shard_map/psum | solution.py:79
  284.6 1.0 copy.146
  285.7 0.6 copy.147
  (92 shorter events, 10.7 us)
Async XLA Ops:
  7.2 63.4 %all-gather.2.cloned.1.call-start = ((), (), s32[]{:S(2)}) async-start(), calls=%async_computation.1 | async-start | bytes 8912896 | tf_op jit(solution)/shard_map/all_gather | solution.py:31
  9.4 221.0 %reduce-scatter.2.cloned.1.call-start = ((), (), s32[]{:S(2)}) async-start(), calls=%async_computation.2 | async-start | bytes 8912896 | tf_op jit(solution)/shard_map/reduce_scatter | solution.py:36
  10.2 66.6 %copy-start.2 = (bf16[32,2,128,128]{3,2,1,0:T(8,128)(2,1)S(1)}, bf16[32,2,128,128]{3,2,1,0:T(8,128)(2,1)}, u32[]{:S(2)}) copy-start(bf16[32,2,128,128]{3,2,1,0:T(8,128)(2,1)} %param.6) | copy-start | bytes 6291460
  76.7 2.8 copy-start
  119.3 0.7 copy-start.8
  119.3 1.1 copy-start.3
  127.5 1.9 copy-start.5
  128.4 2.4 copy-start.4
  129.1 3.2 %collective-permute-start = (bf16[4,2,128,256]{2,3,0,1:T(8,128)(2,1)S(1)}, bf16[4,2,128,256]{2,3,0,1:T(8,128)(2,1)}, u32[]{:S(2)}, u32[]{:S(2)}) collective-permute-start(bf16[4,2,128,256]{2,3,0,1:T(8,128)(2,1)S(1)} %fusion.35), channel_id=1, source_target_pairs={{0,1},{1,0},{2,3},{3,2},{4,5},{5,4},{6,7},{7,6},{8,9},{9,8},{10,11... | collective-permute-start | bytes 1572872 | tf_op jit(solution)/shard_map/ppermute | solution.py:12
  130.9 3.9 %copy-start.6 = (f32[4,1,128,256]{2,3,0,1:T(8,128)S(1)}, f32[4,1,128,256]{2,3,0,1:T(8,128)}, u32[]{:S(2)}) copy-start(f32[4,1,128,256]{2,3,0,1:T(8,128)} %fusion.26) | copy-start | bytes 1572868
  133.9 1.1 copy-start.7
  135.1 19.5 %collective-permute-start.1 = (bf16[4,2,128,256]{2,3,0,1:T(8,128)(2,1)S(1)}, bf16[4,2,128,256]{2,3,0,1:T(8,128)(2,1)}, u32[]{:S(2)}, u32[]{:S(2)}) collective-permute-start(bf16[4,2,128,256]{2,3,0,1:T(8,128)(2,1)S(1)} %fusion.36), channel_id=1, source_target_pairs={{0,2},{1,3},{2,0},{3,1},{4,6},{5,7},{6,4},{7,5},{8,10},{9,11},{10,... | collective-permute-start | bytes 1572872 | tf_op jit(solution)/shard_map/ppermute | solution.py:12
  157.3 31.4 %collective-permute-start.2 = (bf16[4,2,128,256]{2,3,0,1:T(8,128)(2,1)S(1)}, bf16[4,2,128,256]{2,3,0,1:T(8,128)(2,1)S(1)}, u32[]{:S(2)}, u32[]{:S(2)}) collective-permute-start(bf16[4,2,128,256]{2,3,0,1:T(8,128)(2,1)S(1)} %fusion.37), channel_id=1, source_target_pairs={{0,4},{1,5},{2,6},{3,7},{4,0},{5,1},{6,2},{7,3},{8,12},{9,13},{10,... | collective-permute-start | bytes 1572872 | tf_op jit(solution)/shard_map/ppermute | solution.py:12
  190.4 33.7 %collective-permute-start.3 = (bf16[4,2,128,256]{2,3,0,1:T(8,128)(2,1)S(1)}, bf16[4,2,128,256]{2,3,0,1:T(8,128)(2,1)S(1)}, u32[]{:S(2)}, u32[]{:S(2)}) collective-permute-start(bf16[4,2,128,256]{2,3,0,1:T(8,128)(2,1)S(1)} %fusion.38), channel_id=1, source_target_pairs={{0,8},{1,9},{2,10},{3,11},{4,12},{5,13},{6,14},{7,15},{8,0},{9,1},... | collective-permute-start | bytes 1572872 | tf_op jit(solution)/shard_map/ppermute | solution.py:12
  230.4 2.7 copy-start.1
Sparse Core Ops, SparseCore 0:
  10.4 60.1 all-gather.1
  119.4 110.9 reduce-scatter.1
where the time goes:
time: 294 us; the launch traced here: 293 us
  waiting for transfers between devices  143 us (49%)
  blocking collectives  47.5 us (16%)
  local copies, waits for them, and re-layouts  43.1 us (15%)
  matrix products  29.5 us (10%)
  between operations  14.7 us (5%)
  other arithmetic  11.1 us (4%)
  starting transfers between devices  4.59 us (2%)
    ppermute x4, waiting for transfers between devices, swapped(): return lax.ppermute(value, axis, pairs)  77.6 us
    all_gather x1, waiting for transfers between devices, shards(): whole = lax.all_gather(xv, 'rows', axis=0, tiled=True)  60.4 us
    psum x1, blocking collectives, shards(): mean_square = lax.psum(local_orth, 'rows')  24 us
    psum x1, blocking collectives, shards(): proj_re, proj_im = lax.psum((local_re, local_im), 'rows')  23.4 us
    dot_general x52, matrix products, single(): jnp.einsum('sij,sjr->sir', left, right, preferred_element_type=jnp.float32)  17.7 us
    dot_general x1, matrix products, shards(): jnp.einsum('bs,sxyz->bxyz', onehot, prods, precision=lax.Precision.HIGHEST)  11.8 us
    convert_element_type x1, local copies, waits for them, and re-layouts, shards(): jnp.einsum('bs,sxyz->bxyz', onehot, prods, precision=lax.Precision.HIGHEST)  11.4 us
    another operation x1, local copies, waits for them, and re-layouts, complex_blocks(): return jnp.stack([real, imag], axis=1)  10.3 us
  transfers between devices with their start and end apart: 6, of which 5 were waited for; matrix products, arithmetic and copies ran while one was open for 8% of the time, Pallas kernels for 0%

commit v1 on v0

v1 whole, which is shorter than its diff:
```python
import functools

import jax
import jax.numpy as jnp
from jax import lax
from jax.experimental import pallas as pl
from jax.experimental.pallas import tpu as pltpu
from jax.sharding import PartitionSpec as P

LEVELS = 6
REACH = 2
OWN = 28
CHUNKS = 2
F32 = jnp.float32
BF16 = jnp.bfloat16
VMEM = pl.BlockSpec(memory_space=pltpu.VMEM)
SMEM = pl.BlockSpec(memory_space=pltpu.SMEM)


def call(kernel, outs, in_specs, scratch=(), flops=0, bytes_accessed=0, limit=32):
    return pl.pallas_call(
        kernel,
        out_shape=outs,
        grid=(1,),
        in_specs=in_specs,
        out_specs=jax.tree.map(lambda _: VMEM, outs),
        scratch_shapes=list(scratch),
        compiler_params=pltpu.CompilerParams(vmem_limit_bytes=limit * 2**20),
        cost_estimate=pl.CostEstimate(flops=flops, bytes_accessed=bytes_accessed, transcendentals=0),
    )


def mixed(weights, own, picked):
    ur, ui, wr, wi = weights[0], weights[1], weights[2], weights[3]
    real = jnp.concatenate([ur, -ui, wr, -wi], axis=1)
    imag = jnp.concatenate([ui, ur, wi, wr], axis=1)
    left = jnp.concatenate([real, imag], axis=0)
    right = jnp.concatenate([own, picked], axis=0)
    return jnp.dot(left, right, preferred_element_type=F32)


def near_term(block, vector):
    zr, zi = block[0], block[1]
    left = jnp.concatenate(
        [jnp.concatenate([zr, -zi], axis=1), jnp.concatenate([zi, zr], axis=1)], axis=0
    )
    return jnp.dot(left, vector, preferred_element_type=F32)


def prep_kernel(partner, last, weights, low, high, *rest):
    sections, (zero, one) = rest[:-2], rest[-2:]
    blocks = last.shape[1]
    half = blocks // 2
    for b in range(blocks):
        zero[b] = last[0, b].reshape(zero.shape[1:]).astype(BF16)
    low[...] = zero[:half]
    high[...] = zero[half:]
    for b in range(blocks):
        one[b] = mixed(weights[0, b], zero[b], zero[partner[0, b]]).astype(BF16)
    for b in range(blocks):
        done = mixed(weights[1, b], one[b], one[partner[1, b]]).astype(BF16)
        width = done.shape[1] // len(sections)
        for c, section in enumerate(sections):
            section[b] = done[:, c * width : (c + 1) * width]


def level_kernel(level, partner, own, far, weights, out):
    for b in range(own.shape[0]):
        out[b] = mixed(weights[0, b], own[b], far[partner[level, b]]).astype(BF16)


def near_own_kernel(pairs, blocks, before, low, high, after, last, *rest):
    outs, (window, total) = rest[:-2], rest[-2:]
    rows = total.shape[0]
    half = rows // 2
    window[0:half] = before[...]
    window[half : 2 * half] = low[...]
    window[2 * half : 3 * half] = high[...]
    window[3 * half : 4 * half] = after[...]
    first = lax.axis_index("rows") * rows
    for b in range(rows):
        total[b] = last[0, b].reshape(total.shape[1:])

    def body(slot, carry):
        row = pairs[slot, 0] - first
        col = pairs[slot, 1] - first + REACH
        total[row] += near_term(blocks[slot], window[col])
        return carry

    lax.fori_loop(0, OWN, body, 0)
    width = total.shape[2] // len(outs)
    for c, out in enumerate(outs):
        out[...] = total[:, :, c * width : (c + 1) * width]


def near_shipped_kernel(pairs, blocks, before, low, high, after, *rest):
    window = rest[-1]
    count = (len(rest) - 1) // 2
    totals, outs = rest[:count], rest[count : 2 * count]
    rows = totals[0].shape[0]
    half = rows // 2
    entries = blocks.shape[2]
    window[0:half] = before[...]
    window[half : 2 * half] = low[...]
    window[2 * half : 3 * half] = high[...]
    window[3 * half : 4 * half] = after[...]
    first = lax.axis_index("rows") * rows
    for out, total in zip(outs, totals):
        out[...] = total[...]
    width = totals[0].shape[2]

    def body(slot, carry):
        row = pairs[slot, 0] - first
        col = pairs[slot, 1] - first + REACH

        @pl.when((row >= 0) & (row < rows))
        def _():
            block = (blocks[slot, 0:entries], blocks[slot, entries : 2 * entries])
            term = near_term(block, window[col])
            for c, out in enumerate(outs):
                out[row] += term[:, c * width : (c + 1) * width]

        return carry

    lax.fori_loop(0, blocks.shape[0], body, 0)


def gram_kernel(scale, basis, out):
    vectors, blocks = basis.shape[0], basis.shape[1]
    pairs = [(i, j) for i in range(vectors) for j in range(i, vectors)]
    out[...] = jnp.zeros_like(out)
    for b in range(blocks):
        at = 0
        for i, j in pairs:
            ir, ii, jr, ji = basis[i, b, 0], basis[i, b, 1], basis[j, b, 0], basis[j, b, 1]
            out[at : at + 1] += jnp.sum(ir * jr + ii * ji, axis=0, keepdims=True) * scale
            at += 1
            if i != j:
                out[at : at + 1] += jnp.sum(ir * ji - ii * jr, axis=0, keepdims=True) * scale
                at += 1


def project_kernel(level, scale, partner, own, far, weights, base, basis, gram, product, stats):
    vectors, blocks = basis.shape[0], basis.shape[1]
    entries = basis.shape[3]
    sums = [0.0] * (2 * vectors + 1)
    for b in range(blocks):
        section = mixed(weights[0, b], own[b], far[partner[level, b]]).astype(BF16)
        here = base[b] + section.astype(F32)
        product[b] = here
        pr, pi = here[:entries], here[entries:]
        for j in range(vectors):
            br, bi = basis[j, b, 0], basis[j, b, 1]
            sums[j] += jnp.sum(br * pr + bi * pi, axis=0, keepdims=True)
            sums[vectors + j] += jnp.sum(br * pi - bi * pr, axis=0, keepdims=True)
        sums[-1] += jnp.sum(pr * pr + pi * pi, axis=0, keepdims=True)
    used = len(sums)
    for k, value in enumerate(sums):
        stats[k : k + 1] = value * scale
    stats[used : used + gram.shape[0]] = gram[...]
    stats[used + gram.shape[0] :] = jnp.zeros_like(stats[used + gram.shape[0] :])


def finish_kernel(shared, basis, *rest):
    products, (following, coeffs) = rest[:-2], rest[-2:]
    vectors, blocks = basis.shape[0], basis.shape[1]
    entries = basis.shape[3]
    total = shared[0]
    for k in range(1, shared.shape[0]):
        total = total + shared[k]
    hr = [total[j : j + 1] for j in range(vectors)]
    hi = [total[vectors + j : vectors + j + 1] for j in range(vectors)]
    square = total[2 * vectors : 2 * vectors + 1]
    at = 2 * vectors + 1
    for i in range(vectors):
        for j in range(i, vectors):
            gr = total[at : at + 1]
            at += 1
            if i == j:
                square = square + (gr - 2.0) * (hr[i] * hr[i] + hi[i] * hi[i])
            else:
                gi = total[at : at + 1]
                at += 1
                square = square + 2.0 * (
                    gr * (hr[i] * hr[j] + hi[i] * hi[j]) - gi * (hr[i] * hi[j] - hi[i] * hr[j])
                )
    norm = jnp.sqrt(jnp.maximum(square, 0.0) + 1e-06)
    inverse = 1.0 / norm
    for j in range(vectors):
        coeffs[j, 0:1] = hr[j]
        coeffs[j, 1:2] = hi[j]
    coeffs[vectors, 0:1] = norm
    coeffs[vectors, 1:2] = jnp.zeros_like(norm)
    width = products[0].shape[2]
    for c, product in enumerate(products):
        cols = slice(c * width, (c + 1) * width)
        for b in range(blocks):
            real, imag = product[b, :entries], product[b, entries:]
            for j in range(vectors):
                br, bi = basis[j, b, 0, :, cols], basis[j, b, 1, :, cols]
                real = real - (br * hr[j][:, cols] - bi * hi[j][:, cols])
                imag = imag - (br * hi[j][:, cols] + bi * hr[j][:, cols])
            following[b, 0, :, cols] = real * inverse[:, cols]
            following[b, 1, :, cols] = imag * inverse[:, cols]


def swapped(value, mask):
    return lax.ppermute(value, "rows", [(i, i ^ mask) for i in range(lax.axis_size("rows"))])


def shifted(value, step):
    size = lax.axis_size("rows")
    return lax.ppermute(value, "rows", [(i, (i + step) % size) for i in range(size)])


def shards(basis, near_blocks, near_pairs, bfly_weights, partner_local):
    vectors, blocks, _, entries, columns = basis.shape
    size = lax.axis_size("rows")
    half = blocks // 2
    width = columns // CHUNKS
    scale = 1.0 / (size * blocks * entries)
    local_levels = blocks.bit_length() - 1
    shape = jax.ShapeDtypeStruct
    weights_spec = lambda level: pl.BlockSpec(
        (1, blocks, 4, entries, entries), lambda _: (level, 0, 0, 0, 0)
    )
    last_spec = pl.BlockSpec((1, blocks, 2, entries, columns), lambda _: (vectors - 1, 0, 0, 0, 0))

    info = jnp.pad(
        near_pairs[OWN:].astype(BF16)[:, None, :], ((0, 0), (0, 15), (0, entries - 2))
    )
    payload = jnp.concatenate(
        [near_blocks[OWN:].reshape(-1, 2 * entries, entries), info], axis=1
    )
    shipped = lax.all_gather(payload, "rows", axis=0, tiled=True)
    shipped_pairs = shipped[:, 2 * entries, :2].astype(jnp.int32)

    low, high, *sections = call(
        prep_kernel,
        [shape((half, 2 * entries, columns), BF16)] * 2
        + [shape((blocks, 2 * entries, width), BF16)] * CHUNKS,
        [SMEM, last_spec, pl.BlockSpec((2, blocks, 4, entries, entries), lambda _: (0, 0, 0, 0, 0))],
        [pltpu.VMEM((blocks, 2 * entries, columns), BF16)] * 2,
        flops=2 * 16 * blocks * entries * entries * columns,
        bytes_accessed=2**21,
    )(partner_local, basis, bfly_weights)
    before = shifted(high, 1)
    after = shifted(low, -1)

    gram_rows = vectors * vectors
    gram = call(
        functools.partial(gram_kernel, scale),
        shape((gram_rows, columns), F32),
        [VMEM],
        flops=2**23,
        bytes_accessed=2**22,
    )(basis)

    bases = call(
        near_own_kernel,
        [shape((blocks, 2 * entries, width), F32)] * CHUNKS,
        [SMEM, pl.BlockSpec((OWN, 2, entries, entries), lambda _: (0, 0, 0, 0))]
        + [VMEM] * 4
        + [last_spec],
        [
            pltpu.VMEM((2 * blocks, 2 * entries, columns), BF16),
            pltpu.VMEM((blocks, 2 * entries, columns), F32),
        ],
        flops=OWN * 8 * entries * entries * columns,
        bytes_accessed=2**22,
    )(near_pairs, near_blocks, before, low, high, after, basis)

    bases = call(
        near_shipped_kernel,
        [shape((blocks, 2 * entries, width), F32)] * CHUNKS,
        [SMEM] + [VMEM] * (5 + CHUNKS),
        [pltpu.VMEM((2 * blocks, 2 * entries, columns), BF16)],
        flops=2**28,
        bytes_accessed=2**23,
    )(shipped_pairs, shipped, before, low, high, after, *bases)

    for level in range(local_levels, LEVELS - 1):
        mask = 2 ** (level - local_levels)
        sections = [
            call(
                functools.partial(level_kernel, level),
                shape((blocks, 2 * entries, width), BF16),
                [SMEM, VMEM, VMEM, weights_spec(level)],
                flops=16 * blocks * entries * entries * width,
                bytes_accessed=2**20,
            )(partner_local, section, swapped(section, mask), bfly_weights)
            for section in sections
        ]
    level = LEVELS - 1
    mask = 2 ** (level - local_levels)
    stat_rows = -(-(2 * vectors + 1 + gram_rows) // 8) * 8
    products, stats = [], []
    for c, section in enumerate(sections):
        product, stat = call(
            functools.partial(project_kernel, level, scale),
            [shape((blocks, 2 * entries, width), F32), shape((stat_rows, width), F32)],
            [
                SMEM,
                VMEM,
                VMEM,
                weights_spec(level),
                VMEM,
                pl.BlockSpec(
                    (vectors, blocks, 2, entries, width), lambda _, c=c: (0, 0, 0, 0, c)
                ),
                pl.BlockSpec((gram_rows, width), lambda _, c=c: (0, c)),
            ],
            flops=16 * blocks * entries * entries * width,
            bytes_accessed=2**21,
        )(partner_local, section, swapped(section, mask), bfly_weights, bases[c], basis, gram)
        products.append(product)
        stats.append(stat)
    stats = jnp.concatenate(stats, axis=1)
    shared = lax.all_gather(stats, "rows", axis=0)
    following, coeffs = call(
        finish_kernel,
        [
            shape((blocks, 2, entries, columns), F32),
            shape((vectors + 1, 2, columns), F32),
        ],
        [VMEM] * (2 + CHUNKS),
        flops=2**23,
        bytes_accessed=2**23,
    )(shared, basis, *products)
    return following, coeffs


def solution(mesh):
    placed = (
        P("freq", "rows", None, None, None),
        P("rows", "freq", None, None),
        P("rows", None),
        P("freq", "rows", None, None, None),
        P(None, "rows"),
    )
    return jax.shard_map(
        shards,
        mesh=mesh,
        in_specs=placed,
        out_specs=(P("rows", "freq", None, None), P("freq", None, None)),
        check_vma=False,
    )
```

time: 294 us -> 137 us (0.47)
  waiting for transfers between devices: 143 us -> 30.9 us
  matrix products: 29.5 us -> 0 us
  Pallas kernels: 0 us -> 28 us
  local copies, waits for them, and re-layouts: 43.1 us -> 17.3 us
  blocking collectives: 47.5 us -> 30.6 us
  other arithmetic: 11.1 us -> 1.45 us
  starting transfers between devices: 4.59 us -> 13.9 us
    all_gather x1, waiting for transfers between devices: 60.4 us -> 0.01 us  [shards(): shipped = lax.all_gather(payload, 'rows', axis=0, tiled=True)]
    psum x2 -> x0, blocking collectives: 47.5 us -> none  [the longest x1 24 us: shards(): mean_square = lax.psum(local_orth, 'rows')]
    ppermute x4 -> x10, waiting for transfers between devices: 77.6 us -> 30.9 us  [the longest x8 22.5 us: swapped(): lax.ppermute(value, 'rows', [(i, i ^ mask) for i in range(lax.axis_size('...]
    all_gather x0 -> x1, blocking collectives: none -> 30.6 us  [shards(): shared = lax.all_gather(stats, 'rows', axis=0)]
    dot_general x53 -> x0, matrix products: 29.5 us -> none  [the longest x52 17.7 us: single(): jnp.einsum('sij,sjr->sir', left, right, preferred_element_type=jnp.float32)]
    pallas_call x0 -> x13, Pallas kernels: none -> 28 us  [the longest x6 9.84 us: shards(): call(functools.partial(level_kernel, level), shape((blocks, 2 * entries,...]
    convert_element_type x3 -> x1, local copies, waits for them, and re-layouts: 13.5 us -> 0.1 us  [shards(): shipped_pairs = shipped[:, 2 * entries, :2].astype(jnp.int32)]
    gather x7 -> x0, local copies, waits for them, and re-layouts: 12 us -> none  [the longest x1 6.17 us: shards(): prods = complex_blocks(near_blocks, whole[near_pairs[:, 1]])]
  transfers between devices with their start and end apart: 6 -> 11, of which waited for: 5 -> 5; matrix products, arithmetic and copies ran while one was open for 8% -> 1% of each run, Pallas kernels for 0% -> 18%
where the time goes in v1:
time: 137 us; the launch traced here: 136 us
  waiting for transfers between devices  30.9 us (23%)
  blocking collectives  30.6 us (22%)
  Pallas kernels  28 us (20%)
  local copies, waits for them, and re-layouts  17.3 us (13%)
  between operations  14.2 us (10%)
  starting transfers between devices  13.9 us (10%)
  other arithmetic  1.45 us (1%)
    all_gather x1, blocking collectives, shards(): shared = lax.all_gather(stats, 'rows', axis=0)  30.6 us
    ppermute x8, waiting for transfers between devices, swapped(): lax.ppermute(value, 'rows', [(i, i ^ mask) for i in range(lax.axis_size('...  22.5 us
    unnamed x28, local copies, waits for them, and re-layouts  15.2 us
    ppermute x8, starting transfers between devices, swapped(): lax.ppermute(value, 'rows', [(i, i ^ mask) for i in range(lax.axis_size('...  12.9 us
    pallas_call x6, Pallas kernels, shards(): call(functools.partial(level_kernel, level), shape((blocks, 2 * entries,...  9.84 us
    ppermute x2, waiting for transfers between devices, shifted(): lax.ppermute(value, 'rows', [(i, (i + step) % size) for i in range(size)])  8.31 us
    pallas_call x1, Pallas kernels, shards(): call(near_own_kernel, [shape((blocks, 2 * entries, width), F32)] * CHUNKS...  6.77 us
    pallas_call x2, Pallas kernels, shards(): call(functools.partial(project_kernel, level, scale), [shape((blocks, 2 *...  3.49 us
  transfers between devices with their start and end apart: 11, of which 5 were waited for; matrix products, arithmetic and copies ran while one was open for 1% of the time, Pallas kernels for 18%

profile of v1, /device:TPU:1, one launch (start us, length us, event | category | flops | bytes accessed | tf_op | source)
XLA Modules:
  0.0 136.3 jit_solution(14572554154577057048)
XLA Ops:
  7.2 0.0 all-gather.3.cloned.1.call-start
  7.2 1.0 slice.10
  8.2 0.7 convert.4
  8.9 0.1 slice_bitcast_fusion
  8.9 0.1 copy.47
  9.1 0.8 fusion.1
  9.8 0.0 all-gather.3.cloned.1.call-update
  9.8 0.8 copy.41.partner
  10.6 1.9 %copy-done = bf16[6,4,4,128,128]{4,3,2,1,0:T(8,128)(2,1)S(1)} copy-done((bf16[6,4,4,128,128]{4,3,2,1,0:T(8,128)(2,1)S(1)}, bf16[6,4,4,128,128]{4,3,2,1,0:T(8,128)(2,1)}, u32[]{:S(2)}) %copy-start) | copy-done | bytes 3145752
  12.5 2.2 %copy-done.2 = f32[4,4,2,128,256]{4,3,2,1,0:T(8,128)S(1)} copy-done((f32[4,4,2,128,256]{4,3,2,1,0:T(8,128)S(1)}, f32[4,4,2,128,256]{4,3,2,1,0:T(8,128)}, u32[]{:S(2)}) %copy-start.2) | copy-done | bytes 4194328
  14.7 2.1 %shard_map.68 = (bf16[2,256,256]{2,1,0:T(8,128)(2,1)S(1)}, bf16[2,256,256]{2,1,0:T(8,128)(2,1)}, bf16[4,256,128]{2,1,0:T(8,128)(2,1)S(1)}, bf16[4,256,128]{2,1,0:T(8,128)(2,1)S(1)}) custom-call(s32[6,4]{1,0:T(8,128)S(1)} %copy.41.partner, f32[4,4,2,128,256]{4,3,2,1,0:T(8,128)S(1)} %copy-done.2, bf16[6,4,4,128,128]{4,3,2,1,0:T(8,128)(2,1)S(1)} %copy-done), custom_call_target="tpu_custom_call" | custom-call | flops 536870912 | bytes 2097152 | tf_op jit(solution)/shard_map/pallas_call | solution.py:238
  16.8 3.2 %collective-permute-start = (bf16[4,256,128]{2,1,0:T(8,128)(2,1)S(1)}, bf16[4,256,128]{2,1,0:T(8,128)(2,1)S(1)}, u32[]{:S(2)}, u32[]{:S(2)}) collective-permute-start(bf16[4,256,128]{2,1,0:T(8,128)(2,1)S(1)} %get-tuple-element.14.own), channel_id=1, source_target_pairs={{0,1},{1,0},{2,3},{3,2},{4,5},{5,4},{6,7},{7,6},{8,9},{9,8},{10,11... | collective-permute-start | bytes 786440 | tf_op jit(solution)/shard_map/ppermute | solution.py:208
  20.0 1.2 collective-permute-done.far
  21.2 1.0 shard_map.69.own
  22.2 0.1 collective-permute-start.1
  22.3 1.0 shard_map.76.own
  23.3 1.5 %collective-permute-start.7 = (bf16[4,256,128]{2,1,0:T(8,128)(2,1)S(1)}, bf16[4,256,128]{2,1,0:T(8,128)(2,1)S(1)}, u32[]{:S(2)}, u32[]{:S(2)}) collective-permute-start(bf16[4,256,128]{2,1,0:T(8,128)(2,1)S(1)} %shard_map.76.own), channel_id=1, source_target_pairs={{0,2},{1,3},{2,0},{3,1},{4,6},{5,7},{6,4},{7,5},{8,10},{9,11},{10,... | collective-permute-start | bytes 786440 | tf_op jit(solution)/shard_map/ppermute | solution.py:208
  24.9 0.7 collective-permute-start.4
  25.6 0.2 collective-permute-start.5
  25.8 6.6 %collective-permute-done.1.far = bf16[4,256,128]{2,1,0:T(8,128)(2,1)S(1)} collective-permute-done((bf16[4,256,128]{2,1,0:T(8,128)(2,1)S(1)}, bf16[4,256,128]{2,1,0:T(8,128)(2,1)S(1)}, u32[]{:S(2)}, u32[]{:S(2)}) %collective-permute-start.1) | collective-permute-done | bytes 262176 | tf_op jit(solution)/shard_map/ppermute | solution.py:208
  32.4 1.7 %shard_map.70.own = bf16[4,256,128]{2,1,0:T(8,128)(2,1)} custom-call(s32[6,4]{1,0:T(8,128)S(1)} %copy.41.partner, bf16[4,256,128]{2,1,0:T(8,128)(2,1)S(1)} %shard_map.69.own, bf16[4,256,128]{2,1,0:T(8,128)(2,1)S(1)} %collective-permute-done.1.far, bf16[6,4,4,128,128]{4,3,2,1,0:T(8,128)(2,1)S(1)} %copy-done), custom_call_target="tpu_custom_call" | custom-call | flops 134217728 | bytes 1048576 | tf_op jit(solution)/shard_map/pallas_call | solution.py:285
  34.1 1.2 collective-permute-start.2
  35.3 12.7 %collective-permute-done.7.far = bf16[4,256,128]{2,1,0:T(8,128)(2,1)S(1)} collective-permute-done((bf16[4,256,128]{2,1,0:T(8,128)(2,1)S(1)}, bf16[4,256,128]{2,1,0:T(8,128)(2,1)S(1)}, u32[]{:S(2)}, u32[]{:S(2)}) %collective-permute-start.7) | collective-permute-done | bytes 262176 | tf_op jit(solution)/shard_map/ppermute | solution.py:208
  48.0 1.7 %shard_map.77.own = bf16[4,256,128]{2,1,0:T(8,128)(2,1)} custom-call(s32[6,4]{1,0:T(8,128)S(1)} %copy.41.partner, bf16[4,256,128]{2,1,0:T(8,128)(2,1)S(1)} %shard_map.76.own, bf16[4,256,128]{2,1,0:T(8,128)(2,1)S(1)} %collective-permute-done.7.far, bf16[6,4,4,128,128]{4,3,2,1,0:T(8,128)(2,1)S(1)} %copy-done), custom_call_target="tpu_custom_call" | custom-call | flops 134217728 | bytes 1048576 | tf_op jit(solution)/shard_map/pallas_call | solution.py:285
  49.8 0.4 collective-permute-start.8
  50.2 0.1 copy.39.pairs
  50.3 2.2 %copy-done.3 = f32[4,4,2,128,256]{4,3,2,1,0:T(8,128)S(1)} copy-done((f32[4,4,2,128,256]{4,3,2,1,0:T(8,128)S(1)}, f32[4,4,2,128,256]{4,3,2,1,0:T(8,128)}, u32[]{:S(2)}) %copy-start.3) | copy-done | bytes 4194328
  52.5 1.5 %shard_map.74.gram = f32[16,256]{1,0:T(8,128)S(1)} custom-call(f32[4,4,2,128,256]{4,3,2,1,0:T(8,128)S(1)} %copy-done.3), custom_call_target="tpu_custom_call" | custom-call | flops 8388608 | bytes 4194304 | tf_op jit(solution)/shard_map/pallas_call | solution.py:251
  54.0 8.3 %collective-permute-done.5.after = bf16[2,256,256]{2,1,0:T(8,128)(2,1)} collective-permute-done((bf16[2,256,256]{2,1,0:T(8,128)(2,1)S(1)}, bf16[2,256,256]{2,1,0:T(8,128)(2,1)}, u32[]{:S(2)}, u32[]{:S(2)}) %collective-permute-start.5) | collective-permute-done | bytes 262176 | tf_op jit(solution)/shard_map/ppermute | solution.py:213
  62.4 1.6 %copy-done.6 = bf16[32,2,128,128]{3,2,1,0:T(8,128)(2,1)S(1)} copy-done((bf16[32,2,128,128]{3,2,1,0:T(8,128)(2,1)S(1)}, bf16[32,2,128,128]{3,2,1,0:T(8,128)(2,1)}, u32[]{:S(2)}) %copy-start.6) | copy-done | bytes 2097176
  64.0 6.8 %shard_map.72 = (f32[4,256,128]{2,1,0:T(8,128)S(1)}, f32[4,256,128]{2,1,0:T(8,128)S(1)}) custom-call(s32[32,2]{1,0:T(8,128)S(1)} %copy.39.pairs, bf16[32,2,128,128]{3,2,1,0:T(8,128)(2,1)S(1)} %copy-done.6, bf16[2,256,256]{2,1,0:T(8,128)(2,1)} %collective-permute-done.4.before, bf16[2,256,256]{2,1,0:T(8,128)(2,1)S(1)} %get-tuple-element.16.low, ...), custom_call_target="tpu_custom_call" | custom-call | flops 939524096 | bytes 4194304 | tf_op jit(solution)/shard_map/pallas_call | solution.py:259
  70.8 0.8 copy-done.7
  71.5 0.8 copy-done.9
  72.3 2.2 %shard_map.71.own = bf16[4,256,128]{2,1,0:T(8,128)(2,1)} custom-call(s32[6,4]{1,0:T(8,128)S(1)} %copy.41.partner, bf16[4,256,128]{2,1,0:T(8,128)(2,1)} %shard_map.70.own, bf16[4,256,128]{2,1,0:T(8,128)(2,1)} %collective-permute-done.2.far, bf16[6,4,4,128,128]{4,3,2,1,0:T(8,128)(2,1)S(1)} %copy-done.1), custom_call_target="tpu_custom_call" | custom-call | flops 134217728 | bytes 1048576 | tf_op jit(solution)/shard_map/pallas_call | solution.py:285
  74.5 6.5 %collective-permute-start.3 = (bf16[4,256,128]{2,1,0:T(8,128)(2,1)}, bf16[4,256,128]{2,1,0:T(8,128)(2,1)}, u32[]{:S(2)}, u32[]{:S(2)}) collective-permute-start(bf16[4,256,128]{2,1,0:T(8,128)(2,1)} %shard_map.71.own), channel_id=1, source_target_pairs={{0,8},{1,9},{2,10},{3,11},{4,12},{5,13},{6,14},{7,15},{8,0},{9,1},... | collective-permute-start | bytes 786440 | tf_op jit(solution)/shard_map/ppermute | solution.py:208
  81.0 2.2 %shard_map.78.own = bf16[4,256,128]{2,1,0:T(8,128)(2,1)} custom-call(s32[6,4]{1,0:T(8,128)S(1)} %copy.41.partner, bf16[4,256,128]{2,1,0:T(8,128)(2,1)} %shard_map.77.own, bf16[4,256,128]{2,1,0:T(8,128)(2,1)} %collective-permute-done.8.far, bf16[6,4,4,128,128]{4,3,2,1,0:T(8,128)(2,1)S(1)} %copy-done.1), custom_call_target="tpu_custom_call" | custom-call | flops 134217728 | bytes 1048576 | tf_op jit(solution)/shard_map/pallas_call | solution.py:285
  83.2 0.9 slice.13
  84.1 0.1 copy.46
  84.2 0.1 copy.40.pairs
  84.3 2.4 %copy-done.5 = bf16[64,272,128]{2,1,0:T(8,128)(2,1)S(1)} copy-done((bf16[64,272,128]{2,1,0:T(8,128)(2,1)S(1)}, bf16[64,272,128]{2,1,0:T(8,128)(2,1)}, u32[]{:S(2)}) %copy-start.5) | copy-done | bytes 4456472
  86.7 1.2 copy-done.8
  87.9 1.0 copy-done.10
  89.0 2.6 %shard_map.73 = (f32[4,256,128]{2,1,0:T(8,128)S(1)}, f32[4,256,128]{2,1,0:T(8,128)S(1)}) custom-call(s32[64,2]{1,0:T(8,128)S(1)} %copy.40.pairs, bf16[64,272,128]{2,1,0:T(8,128)(2,1)S(1)} %copy-done.5, bf16[2,256,256]{2,1,0:T(8,128)(2,1)} %collective-permute-done.4.before, bf16[2,256,256]{2,1,0:T(8,128)(2,1)S(1)} %get-tuple-element.16.low, ...), custom_call_target="tpu_custom_call" | custom-call | flops 268435456 | bytes 8388608 | tf_op jit(solution)/shard_map/pallas_call | solution.py:273
  91.6 1.7 %shard_map.75 = (f32[4,256,128]{2,1,0:T(8,128)S(1)}, f32[32,128]{1,0:T(8,128)S(1)}) custom-call(s32[6,4]{1,0:T(8,128)S(1)} %copy.41.partner, bf16[4,256,128]{2,1,0:T(8,128)(2,1)} %shard_map.71.own, bf16[4,256,128]{2,1,0:T(8,128)(2,1)} %collective-permute-done.3.far, bf16[6,4,4,128,128]{4,3,2,1,0:T(8,128)(2,1)S(1)} %copy-done.1, ...), custom_call_target="tpu_custom_call" | custom-call | flops 134217728 | bytes 2097152 | tf_op jit(solution)/shard_map/pallas_call | solution.py:299
  93.4 2.0 %collective-permute-done.9.far = bf16[4,256,128]{2,1,0:T(8,128)(2,1)} collective-permute-done((bf16[4,256,128]{2,1,0:T(8,128)(2,1)}, bf16[4,256,128]{2,1,0:T(8,128)(2,1)}, u32[]{:S(2)}, u32[]{:S(2)}) %collective-permute-start.9) | collective-permute-done | bytes 262176 | tf_op jit(solution)/shard_map/ppermute | solution.py:208
  95.4 1.7 %shard_map.79 = (f32[4,256,128]{2,1,0:T(8,128)S(1)}, f32[32,128]{1,0:T(8,128)S(1)}) custom-call(s32[6,4]{1,0:T(8,128)S(1)} %copy.41.partner, bf16[4,256,128]{2,1,0:T(8,128)(2,1)} %shard_map.78.own, bf16[4,256,128]{2,1,0:T(8,128)(2,1)} %collective-permute-done.9.far, bf16[6,4,4,128,128]{4,3,2,1,0:T(8,128)(2,1)S(1)} %copy-done.1, ...), custom_call_target="tpu_custom_call" | custom-call | flops 134217728 | bytes 2097152 | tf_op jit(solution)/shard_map/pallas_call | solution.py:299
  97.2 30.6 %all-gather = f32[512,256]{1,0:T(8,128)S(1)} all-gather(f32[32,256]{1,0:T(8,128)S(1)} %pad_maximum_fusion), channel_id=2, replica_groups=mesh['freq'=16,'rows'=16] {'rows'}, dimensions={0}, use_global_device_ids=true | all-gather | bytes 557056 | tf_op jit(solution)/shard_map/all_gather | solution.py:319
  127.8 1.7 %shard_map.80 = (f32[4,2,128,256]{3,2,1,0:T(8,128)}, f32[5,2,256]{2,1,0:T(2,128)}) custom-call(f32[16,32,256]{2,1,0:T(8,128)S(1)} %bitcast.7, f32[4,4,2,128,256]{4,3,2,1,0:T(8,128)S(1)} %copy-done.4, f32[4,256,128]{2,1,0:T(8,128)S(1)} %get-tuple-element.24.rest_0_, f32[4,256,128]{2,1,0:T(8,128)S(1)} %get-tuple-element.25.rest_1_), custom_call_target="tpu_custom_call" | custom-call | flops 8388608 | bytes 8388608 | tf_op jit(solution)/shard_map/pallas_call | solution.py:320
  (25 shorter events, 0.1 us)
Async XLA Ops:
  7.2 76.0 %all-gather.3.cloned.1.call-start = ((), (), s32[]{:S(2)}) async-start(), calls=%async_computation | async-start | bytes 4734976 | tf_op jit(solution)/shard_map/all_gather | solution.py:235
  10.6 1.9 %copy-start = (bf16[6,4,4,128,128]{4,3,2,1,0:T(8,128)(2,1)S(1)}, bf16[6,4,4,128,128]{4,3,2,1,0:T(8,128)(2,1)}, u32[]{:S(2)}) copy-start(bf16[6,4,4,128,128]{4,3,2,1,0:T(8,128)(2,1)} %weights.17) | copy-start | bytes 9437188
  12.5 2.2 %copy-start.2 = (f32[4,4,2,128,256]{4,3,2,1,0:T(8,128)S(1)}, f32[4,4,2,128,256]{4,3,2,1,0:T(8,128)}, u32[]{:S(2)}) copy-start(f32[4,4,2,128,256]{4,3,2,1,0:T(8,128)} %basis.7) | copy-start | bytes 12582916
  16.8 4.4 %collective-permute-start = (bf16[4,256,128]{2,1,0:T(8,128)(2,1)S(1)}, bf16[4,256,128]{2,1,0:T(8,128)(2,1)S(1)}, u32[]{:S(2)}, u32[]{:S(2)}) collective-permute-start(bf16[4,256,128]{2,1,0:T(8,128)(2,1)S(1)} %get-tuple-element.14.own), channel_id=1, source_target_pairs={{0,1},{1,0},{2,3},{3,2},{4,5},{5,4},{6,7},{7,6},{8,9},{9,8},{10,11... | collective-permute-start | bytes 786440 | tf_op jit(solution)/shard_map/ppermute | solution.py:208
  20.0 2.3 %collective-permute-start.6 = (bf16[4,256,128]{2,1,0:T(8,128)(2,1)S(1)}, bf16[4,256,128]{2,1,0:T(8,128)(2,1)S(1)}, u32[]{:S(2)}, u32[]{:S(2)}) collective-permute-start(bf16[4,256,128]{2,1,0:T(8,128)(2,1)S(1)} %get-tuple-element.21.own), channel_id=1, source_target_pairs={{0,1},{1,0},{2,3},{3,2},{4,5},{5,4},{6,7},{7,6},{8,9},{9,8},{10,11... | collective-permute-start | bytes 786440 | tf_op jit(solution)/shard_map/ppermute | solution.py:208
  22.2 10.2 %collective-permute-start.1 = (bf16[4,256,128]{2,1,0:T(8,128)(2,1)S(1)}, bf16[4,256,128]{2,1,0:T(8,128)(2,1)S(1)}, u32[]{:S(2)}, u32[]{:S(2)}) collective-permute-start(bf16[4,256,128]{2,1,0:T(8,128)(2,1)S(1)} %shard_map.69.own), channel_id=1, source_target_pairs={{0,2},{1,3},{2,0},{3,1},{4,6},{5,7},{6,4},{7,5},{8,10},{9,11},{10,... | collective-permute-start | bytes 786440 | tf_op jit(solution)/shard_map/ppermute | solution.py:208
  23.3 26.9 %copy-start.11 = (s32[32,2]{0,1:T(2,128)S(1)}, s32[32,2]{0,1:T(2,128)}, u32[]{:S(2)}) copy-start(s32[32,2]{0,1:T(2,128)} %param.7) | copy-start | bytes 772
  23.3 24.7 %collective-permute-start.7 = (bf16[4,256,128]{2,1,0:T(8,128)(2,1)S(1)}, bf16[4,256,128]{2,1,0:T(8,128)(2,1)S(1)}, u32[]{:S(2)}, u32[]{:S(2)}) collective-permute-start(bf16[4,256,128]{2,1,0:T(8,128)(2,1)S(1)} %shard_map.76.own), channel_id=1, source_target_pairs={{0,2},{1,3},{2,0},{3,1},{4,6},{5,7},{6,4},{7,5},{8,10},{9,11},{10,... | collective-permute-start | bytes 786440 | tf_op jit(solution)/shard_map/ppermute | solution.py:208
  24.9 29.2 %collective-permute-start.4 = (bf16[2,256,256]{2,1,0:T(8,128)(2,1)}, bf16[2,256,256]{2,1,0:T(8,128)(2,1)}, u32[]{:S(2)}, u32[]{:S(2)}) collective-permute-start(bf16[2,256,256]{2,1,0:T(8,128)(2,1)} %get-tuple-element.15.high), channel_id=1, source_target_pairs={{0,1},{1,2},{2,3},{3,4},{4,5},{5,6},{6,7},{7,8},{8,9},{9,10},{10,1... | collective-permute-start | bytes 786440 | tf_op jit(solution)/shard_map/ppermute | solution.py:213
  25.6 36.8 %collective-permute-start.5 = (bf16[2,256,256]{2,1,0:T(8,128)(2,1)S(1)}, bf16[2,256,256]{2,1,0:T(8,128)(2,1)}, u32[]{:S(2)}, u32[]{:S(2)}) collective-permute-start(bf16[2,256,256]{2,1,0:T(8,128)(2,1)S(1)} %get-tuple-element.16.low), channel_id=1, source_target_pairs={{0,15},{1,0},{2,1},{3,2},{4,3},{5,4},{6,5},{7,6},{8,7},{9,8},{10,9... | collective-permute-start | bytes 786440 | tf_op jit(solution)/shard_map/ppermute | solution.py:213
  34.1 38.2 %collective-permute-start.2 = (bf16[4,256,128]{2,1,0:T(8,128)(2,1)}, bf16[4,256,128]{2,1,0:T(8,128)(2,1)}, u32[]{:S(2)}, u32[]{:S(2)}) collective-permute-start(bf16[4,256,128]{2,1,0:T(8,128)(2,1)} %shard_map.70.own), channel_id=1, source_target_pairs={{0,4},{1,5},{2,6},{3,7},{4,0},{5,1},{6,2},{7,3},{8,12},{9,13},{10,... | collective-permute-start | bytes 786440 | tf_op jit(solution)/shard_map/ppermute | solution.py:208
  49.8 31.2 %collective-permute-start.8 = (bf16[4,256,128]{2,1,0:T(8,128)(2,1)}, bf16[4,256,128]{2,1,0:T(8,128)(2,1)}, u32[]{:S(2)}, u32[]{:S(2)}) collective-permute-start(bf16[4,256,128]{2,1,0:T(8,128)(2,1)} %shard_map.77.own), channel_id=1, source_target_pairs={{0,4},{1,5},{2,6},{3,7},{4,0},{5,1},{6,2},{7,3},{8,12},{9,13},{10,... | collective-permute-start | bytes 786440 | tf_op jit(solution)/shard_map/ppermute | solution.py:208
  50.3 2.2 %copy-start.3 = (f32[4,4,2,128,256]{4,3,2,1,0:T(8,128)S(1)}, f32[4,4,2,128,256]{4,3,2,1,0:T(8,128)}, u32[]{:S(2)}) copy-start(f32[4,4,2,128,256]{4,3,2,1,0:T(8,128)} %basis.7) | copy-start | bytes 12582916
  54.0 18.3 %copy-start.1 = (bf16[6,4,4,128,128]{4,3,2,1,0:T(8,128)(2,1)S(1)}, bf16[6,4,4,128,128]{4,3,2,1,0:T(8,128)(2,1)}, u32[]{:S(2)}) copy-start(bf16[6,4,4,128,128]{4,3,2,1,0:T(8,128)(2,1)} %weights.17) | copy-start | bytes 9437188
  62.4 1.6 %copy-start.6 = (bf16[32,2,128,128]{3,2,1,0:T(8,128)(2,1)S(1)}, bf16[32,2,128,128]{3,2,1,0:T(8,128)(2,1)}, u32[]{:S(2)}) copy-start(bf16[32,2,128,128]{3,2,1,0:T(8,128)(2,1)} %blocks.1) | copy-start | bytes 6291460
  70.7 0.8 copy-start.7
  71.5 0.8 copy-start.9
  74.5 17.1 %collective-permute-start.3 = (bf16[4,256,128]{2,1,0:T(8,128)(2,1)}, bf16[4,256,128]{2,1,0:T(8,128)(2,1)}, u32[]{:S(2)}, u32[]{:S(2)}) collective-permute-start(bf16[4,256,128]{2,1,0:T(8,128)(2,1)} %shard_map.71.own), channel_id=1, source_target_pairs={{0,8},{1,9},{2,10},{3,11},{4,12},{5,13},{6,14},{7,15},{8,0},{9,1},... | collective-permute-start | bytes 786440 | tf_op jit(solution)/shard_map/ppermute | solution.py:208
  83.2 12.3 %collective-permute-start.9 = (bf16[4,256,128]{2,1,0:T(8,128)(2,1)}, bf16[4,256,128]{2,1,0:T(8,128)(2,1)}, u32[]{:S(2)}, u32[]{:S(2)}) collective-permute-start(bf16[4,256,128]{2,1,0:T(8,128)(2,1)} %shard_map.78.own), channel_id=1, source_target_pairs={{0,8},{1,9},{2,10},{3,11},{4,12},{5,13},{6,14},{7,15},{8,0},{9,1},... | collective-permute-start | bytes 786440 | tf_op jit(solution)/shard_map/ppermute | solution.py:208
  84.3 7.3 %copy-start.4 = (f32[4,4,2,128,256]{4,3,2,1,0:T(8,128)S(1)}, f32[4,4,2,128,256]{4,3,2,1,0:T(8,128)}, u32[]{:S(2)}) copy-start(f32[4,4,2,128,256]{4,3,2,1,0:T(8,128)} %basis.7) | copy-start | bytes 12582916
  84.3 2.4 %copy-start.5 = (bf16[64,272,128]{2,1,0:T(8,128)(2,1)S(1)}, bf16[64,272,128]{2,1,0:T(8,128)(2,1)}, u32[]{:S(2)}) copy-start(bf16[64,272,128]{2,1,0:T(8,128)(2,1)} %all-gather.3.cloned.1.call-done.blocks) | copy-start | bytes 13369348
  86.7 1.2 copy-start.8
  87.9 1.0 copy-start.10
Sparse Core Ops, SparseCore 0:
  10.0 65.2 all-gather.2

commit v2 on v1

v2 whole, which is shorter than its diff:
```python
import functools

import jax
import jax.numpy as jnp
from jax import lax
from jax.experimental import pallas as pl
from jax.experimental.pallas import tpu as pltpu
from jax.sharding import PartitionSpec as P

LEVELS = 6
REACH = 2
OWN = 28
CHUNKS = 2
F32 = jnp.float32
BF16 = jnp.bfloat16
VMEM = pl.BlockSpec(memory_space=pltpu.VMEM)
SMEM = pl.BlockSpec(memory_space=pltpu.SMEM)
HBM = pl.BlockSpec(memory_space=pltpu.HBM)
ANY = pl.BlockSpec(memory_space=pl.ANY)
EXTRA = 32
INFO = 8
BIG = 60
RING, NEAR, HALO = ("ring", 0), ("near", 0), ("halo", 0)
PLAN = [(3, 0), HALO, (3, 1), RING, NEAR, RING, (4, 0), RING, (4, 1)]
COSTLY = 2 * 10**10


def call(kernel, outs, in_specs, scratch=(), limit=16, after=(), cost=1):
    run = pl.pallas_call(
        kernel,
        out_shape=outs,
        in_specs=list(in_specs) + [ANY] * len(after),
        out_specs=jax.tree.map(lambda _: VMEM, outs),
        scratch_shapes=list(scratch),
        compiler_params=pltpu.CompilerParams(vmem_limit_bytes=limit * 2**20),
        cost_estimate=pl.CostEstimate(flops=cost, bytes_accessed=1, transcendentals=0),
    )
    return lambda *operands: run(*operands, *after)


def mixed(weights, own, picked):
    ur, ui, wr, wi = weights[0], weights[1], weights[2], weights[3]
    real = jnp.concatenate([ur, -ui, wr, -wi], axis=1)
    imag = jnp.concatenate([ui, ur, wi, wr], axis=1)
    left = jnp.concatenate([real, imag], axis=0)
    right = jnp.concatenate([own, picked], axis=0)
    return jnp.dot(left, right, preferred_element_type=F32)


def near_term(zr, zi, vector):
    left = jnp.concatenate(
        [jnp.concatenate([zr, -zi], axis=1), jnp.concatenate([zi, zr], axis=1)], axis=0
    )
    return jnp.dot(left, vector, preferred_element_type=F32)


def gather_kernel(scale, pairs, blocks, source, *rest):
    out, basis, gram, slot_sem, basis_sem = rest[-5:]
    count, rows, lanes = out.shape
    entries = (rows - EXTRA) // 2
    vectors, nblocks = basis.shape[0], basis.shape[1]
    columns = basis.shape[-1]
    copies = [
        pltpu.make_async_copy(source.at[:, b], basis.at[:, b], basis_sem.at[b])
        for b in range(nblocks)
    ]
    get_slots = [
        pltpu.make_async_copy(
            blocks.at[OWN + k, part],
            out.at[k, pl.ds(part * entries, entries)],
            slot_sem.at[k, part],
        )
        for k in range(count)
        for part in range(2)
    ]
    for copy in copies + get_slots:
        copy.start()
    gram[...] = jnp.zeros_like(gram)
    for b, copy in enumerate(copies):
        copy.wait()
        at = 0
        for i in range(vectors):
            ir, ii = basis[i, b, 0], basis[i, b, 1]
            for j in range(i, vectors):
                jr, ji = basis[j, b, 0], basis[j, b, 1]
                gram[at : at + 1] += jnp.sum(ir * jr + ii * ji, axis=0, keepdims=True) * scale
                at += 1
                if i != j:
                    gram[at : at + 1] += jnp.sum(ir * ji - ii * jr, axis=0, keepdims=True) * scale
                    at += 1
    whole = jnp.concatenate(
        [gram[:, c * lanes : (c + 1) * lanes] for c in range(columns // lanes)], axis=0
    )
    top = whole.astype(BF16).astype(F32)
    middle = (whole - top).astype(BF16).astype(F32)
    parts = jnp.concatenate([top, middle, whole - top - middle], axis=0)
    share = parts.shape[0] // count
    lane = lax.broadcasted_iota(jnp.int32, (INFO, lanes), 1)
    for k in range(count):
        place = jnp.where(lane == 0, pairs[0, OWN + k], jnp.where(lane == 1, pairs[1, OWN + k], 0))
        tile = [parts[k * share : (k + 1) * share], place.astype(F32)]
        out[k, 2 * entries :] = jnp.concatenate(tile, axis=0).astype(BF16)
    for copy in get_slots:
        copy.wait()


def prep_kernel(partner, basis, all_weights, low, high, *rest):
    sections, (last, weights, zero, one, last_sem, weight_sem) = rest[:-6], rest[-6:]
    blocks = last.shape[0]
    half = blocks // 2
    get_last = [
        pltpu.make_async_copy(basis.at[basis.shape[0] - 1, b], last.at[b], last_sem.at[b])
        for b in range(blocks)
    ]
    get_weights = [
        pltpu.make_async_copy(all_weights.at[level], weights.at[level], weight_sem.at[level])
        for level in range(2)
    ]
    for copy in get_last:
        copy.start()
    for copy in get_weights:
        copy.start()
    for b in range(blocks):
        get_last[b].wait()
        zero[b] = last[b].reshape(zero.shape[1:]).astype(BF16)
    low[...] = zero[:half]
    high[...] = zero[half:]
    get_weights[0].wait()
    for b in range(blocks):
        one[b] = mixed(weights[0, b], zero[b], zero[partner[b, 0]]).astype(BF16)
    get_weights[1].wait()
    for b in range(blocks):
        done = mixed(weights[1, b], one[b], one[partner[b, 1]]).astype(BF16)
        width = done.shape[1] // len(sections)
        for c, section in enumerate(sections):
            section[b] = done[:, c * width : (c + 1) * width]


def level_kernel(level, partner, own, far, weights, *rest):
    out = rest[-1]
    for b in range(own.shape[0]):
        out[b] = mixed(weights[level, b], own[b], far[partner[b, level]]).astype(BF16)


def near_own_kernel(pairs, near_blocks, before, low, high, after, basis, *rest):
    outs = rest[-6 - CHUNKS : -6]
    window, total, blocks, window_sem, last_sem, block_sem = rest[-6:]
    rows, _, entries, columns = total.shape
    half = rows // 2
    group = OWN // block_sem.shape[0]
    copies = [
        pltpu.make_async_copy(part, window.at[pl.ds(k * half, half)], window_sem.at[k])
        for k, part in enumerate((before, low, high, after))
    ]
    copies.append(pltpu.make_async_copy(basis.at[basis.shape[0] - 1], total, last_sem))
    get_blocks = [
        pltpu.make_async_copy(
            near_blocks.at[pl.ds(g * group, group)],
            blocks.at[pl.ds(g * group, group)],
            block_sem.at[g],
        )
        for g in range(block_sem.shape[0])
    ]
    for copy in copies + get_blocks:
        copy.start()
    for copy in copies:
        copy.wait()
    first = lax.axis_index("rows") * rows

    for g, copy in enumerate(get_blocks):
        copy.wait()
        for slot in range(g * group, (g + 1) * group):
            row = pairs[0, slot] - first
            col = pairs[1, slot] - first + REACH
            term = near_term(blocks[slot, 0], blocks[slot, 1], window[col])
            total[row] += term.reshape(2, entries, columns)
    width = columns // len(outs)
    for c, out in enumerate(outs):
        for b in range(rows):
            out[b] = total[b, :, :, c * width : (c + 1) * width].reshape(2 * entries, width)


def slot_offset(shipped, away, flip, skip):
    device = lax.axis_index("rows")
    chips = lax.axis_size("rows") // 2
    chip, core = device // 2, device % 2
    chip = lax.rem(chip + away * (2 * core - 1) + 2 * chips, chips)
    return (chip * 2 + (core ^ flip)) * shipped + skip


def near_shipped_kernel(places, shares, shipped, before, low, high, after, *rest):
    count = len(places)
    pieces = rest[:count]
    totals = rest[count : count + CHUNKS]
    scratch = 8 if shares else 7
    window, blocks, table, pairs, window_sem, piece_sem, table_sem = rest[-7:]
    outs = rest[-scratch - 1 - CHUNKS : -scratch - 1] if shares else rest[-7 - CHUNKS : -7]
    rows, _, width = totals[0].shape
    half = rows // 2
    entries = (blocks.shape[1] - EXTRA) // 2
    copies = [
        pltpu.make_async_copy(part, window.at[pl.ds(k * half, half)], window_sem.at[k])
        for k, part in enumerate((before, low, high, after))
    ]
    used = 0
    for k, (piece, (away, flip, start, size, skip, whole)) in enumerate(zip(pieces, places)):
        if whole:
            copies.append(
                pltpu.make_async_copy(
                    piece.at[pl.ds(start, size)], blocks.at[pl.ds(used, size)], piece_sem.at[k]
                )
            )
            used += size
        if shares:
            at = slot_offset(shipped, away, flip, skip)
            copies.append(
                pltpu.make_async_copy(
                    piece.at[pl.ds(start, size), pl.ds(2 * entries, EXTRA)],
                    rest[-8].at[pl.ds(at, size)],
                    piece_sem.at[count + k],
                )
            )
    for copy in copies:
        copy.start()
    first = lax.axis_index("rows") * rows
    for out, total in zip(outs, totals):
        out[...] = total[...]
    for copy in copies:
        copy.wait()
    below = blocks[:, 2 * entries + EXTRA - INFO :].astype(F32)
    table[...] = jnp.max(below, axis=1).astype(jnp.int32)
    copy = pltpu.make_async_copy(table, pairs, table_sem)
    copy.start()
    if shares:
        gram, below = rest[-9], rest[-8][:, : EXTRA - INFO].astype(F32)
        parts = []
        for k in range(shipped):
            part = below[k]
            for d in range(1, below.shape[0] // shipped):
                part = part + below[d * shipped + k]
            parts.append(part)
        parts = jnp.concatenate(parts, axis=0)
        whole = parts.shape[0] // 3
        parts = parts[:whole] + (parts[whole : 2 * whole] + parts[2 * whole :])
        lanes, high_rows = parts.shape[1], gram.shape[0]
        for c in range(gram.shape[1] // lanes):
            gram[:, c * lanes : (c + 1) * lanes] = parts[c * high_rows : (c + 1) * high_rows]
    copy.wait()

    def body(slot, carry):
        row = pairs[slot, 0] - first
        col = pairs[slot, 1] - first + REACH

        @pl.when((row >= 0) & (row < rows))
        def _():
            term = near_term(
                blocks[slot, 0:entries], blocks[slot, entries : 2 * entries], window[col]
            )
            for c, out in enumerate(outs):
                out[row] += term[:, c * width : (c + 1) * width]

        return carry

    lax.fori_loop(0, used, body, 0)


def project_kernel(level, chunk, scale, partner, own, far, weights, base, basis, *rest):
    product, stats = rest[-2:]
    vectors, blocks = basis.shape[0], basis.shape[1]
    entries = basis.shape[3]
    width = own.shape[2]
    cols = slice(chunk * width, (chunk + 1) * width)
    sums = [0.0] * (2 * vectors + 1)
    for b in range(blocks):
        section = mixed(weights[level, b], own[b], far[partner[b, level]]).astype(BF16)
        here = base[b] + section.astype(F32)
        product[b] = here
        pr, pi = here[:entries], here[entries:]
        for j in range(vectors):
            br, bi = basis[j, b, 0, :, cols], basis[j, b, 1, :, cols]
            sums[j] += jnp.sum(br * pr + bi * pi, axis=0, keepdims=True)
            sums[vectors + j] += jnp.sum(br * pi - bi * pr, axis=0, keepdims=True)
        sums[-1] += jnp.sum(pr * pr + pi * pi, axis=0, keepdims=True)
    for k, value in enumerate(sums):
        stats[k : k + 1] = value * scale


def finish_kernel(shared, gram, basis, *rest):
    products, (following, coeffs) = rest[:-2], rest[-2:]
    vectors, blocks = basis.shape[0], basis.shape[1]
    entries = basis.shape[3]
    total = shared[0]
    for k in range(1, shared.shape[0]):
        total = total + shared[k]
    each = 2 * vectors + 1
    whole = [
        jnp.concatenate([total[c * each + k : c * each + k + 1] for c in range(len(products))], axis=1)
        for k in range(each)
    ]
    hr, hi, square = whole[:vectors], whole[vectors : 2 * vectors], whole[-1]
    at = 0
    for i in range(vectors):
        for j in range(i, vectors):
            gr = gram[at : at + 1]
            at += 1
            if i == j:
                square = square + (gr - 2.0) * (hr[i] * hr[i] + hi[i] * hi[i])
            else:
                gi = gram[at : at + 1]
                at += 1
                square = square + 2.0 * (
                    gr * (hr[i] * hr[j] + hi[i] * hi[j]) - gi * (hr[i] * hi[j] - hi[i] * hr[j])
                )
    norm = jnp.sqrt(jnp.maximum(square, 0.0) + 1e-06)
    inverse = 1.0 / norm
    for j in range(vectors):
        coeffs[j, 0:1] = hr[j]
        coeffs[j, 1:2] = hi[j]
    coeffs[vectors, 0:1] = norm
    coeffs[vectors, 1:2] = jnp.zeros_like(norm)
    width = products[0].shape[2]
    for c, product in enumerate(products):
        cols = slice(c * width, (c + 1) * width)
        for b in range(blocks):
            real, imag = product[b, :entries], product[b, entries:]
            for j in range(vectors):
                br, bi = basis[j, b, 0, :, cols], basis[j, b, 1, :, cols]
                real = real - (br * hr[j][:, cols] - bi * hi[j][:, cols])
                imag = imag - (br * hi[j][:, cols] + bi * hr[j][:, cols])
            following[b, 0, :, cols] = real * inverse[:, cols]
            following[b, 1, :, cols] = imag * inverse[:, cols]


def swapped(value, mask):
    return lax.ppermute(value, "rows", [(i, i ^ mask) for i in range(lax.axis_size("rows"))])


def shifted(value, step):
    size = lax.axis_size("rows")
    return lax.ppermute(value, "rows", [(i, (i + step) % size) for i in range(size)])


def around(value):
    size = lax.axis_size("rows")
    return lax.ppermute(
        value, "rows", [(i, (i + (2 if i % 2 == 0 else -2)) % size) for i in range(size)]
    )


def behind(value, *others):
    return lax.optimization_barrier((value,) + others)[0]


def shards(basis, near_blocks, near_pairs, bfly_weights, partner_local):
    vectors, blocks, _, entries, columns = basis.shape
    size = lax.axis_size("rows")
    chips = size // 2
    half = blocks // 2
    width = columns // CHUNKS
    shipped = near_pairs.shape[0] - OWN
    scale = 1.0 / (size * blocks * entries)
    local_levels = blocks.bit_length() - 1
    shape = jax.ShapeDtypeStruct
    dma = pltpu.SemaphoreType.DMA
    pairs = near_pairs.T
    partner = partner_local.T

    low, high, *sections = call(
        prep_kernel,
        [shape((half, 2 * entries, columns), BF16)] * 2
        + [shape((blocks, 2 * entries, width), BF16)] * CHUNKS,
        [SMEM, HBM, HBM],
        [
            pltpu.VMEM((blocks, 2, entries, columns), F32),
            pltpu.VMEM((2, blocks, 4, entries, entries), BF16),
            pltpu.VMEM((blocks, 2 * entries, columns), BF16),
            pltpu.VMEM((blocks, 2 * entries, columns), BF16),
            dma((blocks,)),
            dma((2,)),
        ],
        limit=BIG,
    )(partner, basis, bfly_weights)

    def exchanged(level, c):
        return swapped(sections[c], 2 ** (level - local_levels))

    def level_step(level, c, far, *after):
        return call(
            functools.partial(level_kernel, level),
            shape((blocks, 2 * entries, width), BF16),
            [SMEM, VMEM, VMEM, VMEM],
            after=after,
            cost=COSTLY,
        )(partner, sections[c], far, bfly_weights)

    far = [exchanged(local_levels, c) for c in range(CHUNKS)]
    order = sections[0] = level_step(local_levels, 0, far[0])
    far[0] = exchanged(local_levels + 1, 0)

    gram_rows = vectors * vectors
    own_slots, held = call(
        functools.partial(gather_kernel, scale),
        [shape((shipped, 2 * entries + EXTRA, entries), BF16), shape(basis.shape, F32)],
        [SMEM, HBM, HBM],
        [pltpu.VMEM((gram_rows, columns), F32), dma((shipped, 2)), dma((blocks,))],
        after=(order,),
        cost=COSTLY,
    )(pairs, near_blocks, basis)
    other_slots = swapped(own_slots, 1)

    order = own_slots
    for c in range(1, CHUNKS):
        order = sections[c] = level_step(local_levels, c, far[c], order)
        far[c] = exchanged(local_levels + 1, c)

    steps = chips // 2
    order = behind(jnp.concatenate([own_slots, other_slots], axis=0), order)
    pieces, theirs = [around(order)], []
    theirs.append(swapped(pieces[0], 1))

    def ring_step(order):
        piece = behind(pieces[-1], order, *theirs[:-1])
        if len(pieces) < steps - 1:
            pieces.append(around(piece))
            theirs.append(swapped(pieces[-1], 1))
        else:
            pieces.append(around(piece[:shipped]))
        return piece

    for level, c in PLAN:
        if level == "ring":
            order = ring_step(order)
        elif level == "halo":
            before = shifted(behind(high, order), 1)
            after = shifted(behind(low, order), -1)
        elif level == "near":
            bases = call(
                near_own_kernel,
                [shape((blocks, 2 * entries, width), F32)] * CHUNKS,
                [SMEM, HBM] + [ANY] * 4 + [HBM],
                [
                    pltpu.VMEM((2 * blocks, 2 * entries, columns), BF16),
                    pltpu.VMEM((blocks, 2, entries, columns), F32),
                    pltpu.VMEM((OWN, 2, entries, entries), BF16),
                    dma((4,)),
                    dma,
                    dma((4,)),
                ],
                after=(order,),
                cost=COSTLY,
            )(pairs, near_blocks, before, low, high, after, basis)
            order = bases[0]
        else:
            order = sections[c] = level_step(level, c, far[c], order)
            far[c] = exchanged(level + 1, c)

    early = [(own_slots, (0, 0, 0, shipped, 0)), (other_slots, (0, 1, 0, shipped, 0))]
    for k in range(steps - 1):
        for flip in range(2):
            part = flip * shipped
            early.append((pieces[k], (k + 1, flip, part, shipped, 0)))
            early.append((theirs[k], (-(k + 1), 1 - flip, part, shipped, 0)))
    def near_shipped(sources, others, order, bases):
        shares = len(others) > 0
        used = sum(place[3] for _, place in sources)
        places = [place + (True,) for _, place in sources] + [place + (False,) for _, place in others]
        every = [source for source, _ in sources + others]
        return call(
            functools.partial(near_shipped_kernel, places, shares, shipped),
            [shape((blocks, 2 * entries, width), F32)] * CHUNKS
            + [shape((gram_rows, columns), F32)] * shares,
            [ANY] * (4 + len(every)) + [VMEM] * CHUNKS,
            [pltpu.VMEM((size * shipped, EXTRA, entries), BF16)] * shares
            + [
                pltpu.VMEM((2 * blocks, 2 * entries, columns), BF16),
                pltpu.VMEM((used, 2 * entries + EXTRA, entries), BF16),
                pltpu.VMEM((used, entries), jnp.int32),
                pltpu.SMEM((used, entries), jnp.int32),
                dma((4,)),
                dma((2 * len(every),)),
                dma,
            ],
            after=(order,),
        )(before, low, high, after, *every, *bases)

    bases = near_shipped(early, [], order, bases)
    late = [(pieces[-1], (steps, 0, 0, shipped, 0))]
    for k, part in enumerate(jnp.split(behind(pieces[-1], bases[0]), 2)):
        late.append((swapped(part, 1), (steps, 1, 0, shipped // 2, k * (shipped // 2))))
    *bases, gram = near_shipped(late, early, far[0], bases)

    level = LEVELS - 1
    each = 2 * vectors + 1
    products, stats = [], []
    for c in range(CHUNKS):
        product, stat = call(
            functools.partial(project_kernel, level, c, scale),
            [shape((blocks, 2 * entries, width), F32), shape((each, width), F32)],
            [SMEM] + [VMEM] * 5,
            after=tuple(stats),
        )(partner, sections[c], far[c], bfly_weights, bases[c], held)
        products.append(product)
        stats.append(stat)
    stats = jnp.concatenate(stats, axis=0)
    shared = lax.all_to_all(jnp.broadcast_to(stats, (size,) + stats.shape), "rows", 0, 0)
    following, coeffs = call(
        finish_kernel,
        [
            shape((blocks, 2, entries, columns), F32),
            shape((vectors + 1, 2, columns), F32),
        ],
        [VMEM] * (3 + CHUNKS),
    )(shared, gram, held, *products)
    return following, coeffs


def solution(mesh):
    placed = (
        P("freq", "rows", None, None, None),
        P("rows", "freq", None, None),
        P("rows", None),
        P("freq", "rows", None, None, None),
        P(None, "rows"),
    )
    return jax.shard_map(
        shards,
        mesh=mesh,
        in_specs=placed,
        out_specs=(P("rows", "freq", None, None), P("freq", None, None)),
        check_vma=False,
    )
```

time: 137 us -> 120 us (0.88)
  starting transfers between devices: 13.9 us -> 43.9 us
  local copies, waits for them, and re-layouts: 17.3 us -> 1.54 us
  between operations: 14.2 us -> 0.89 us
  blocking collectives: 30.6 us -> 20.4 us
  waiting for transfers between devices: 30.9 us -> 25.8 us
  other arithmetic: 1.45 us -> 0.06 us
    all_gather x1 -> x0, blocking collectives: 30.6 us -> none  [shards(): shared = lax.all_gather(stats, 'rows', axis=0)]
    ppermute x0 -> x4, waiting for transfers between devices: none -> 23.4 us  [around(): lax.ppermute(value, 'rows', [(i, (i + (2 if i % 2 == 0 else -2)) % size)...]
    all_to_all x0 -> x1, blocking collectives: none -> 20.4 us  [shards(): lax.all_to_all(jnp.broadcast_to(stats, (size,) + stats.shape), 'rows', 0, 0)]
    ppermute x8 -> x14, waiting for transfers between devices: 22.5 us -> 2.33 us  [swapped(): lax.ppermute(value, 'rows', [(i, i ^ mask) for i in range(lax.axis_size('...]
    ppermute x8 -> x14, starting transfers between devices: 12.9 us -> 31.7 us  [swapped(): lax.ppermute(value, 'rows', [(i, i ^ mask) for i in range(lax.axis_size('...]
    unnamed x28 -> x18, local copies, waits for them, and re-layouts: 15.2 us -> 1.49 us
    ppermute x0 -> x4, starting transfers between devices: none -> 9.35 us  [around(): lax.ppermute(value, 'rows', [(i, (i + (2 if i % 2 == 0 else -2)) % size)...]
    ppermute x2, waiting for transfers between devices: 8.31 us -> 0.01 us  [shifted(): lax.ppermute(value, 'rows', [(i, (i + step) % size) for i in range(size)])]
  transfers between devices with their start and end apart: 11 -> 20, of which waited for: 5 -> 6; matrix products, arithmetic and copies ran while one was open for 1% -> 0% of each run, Pallas kernels for 18% -> 17%
where the time goes in v2:
time: 120 us
  starting transfers between devices  43.9 us (37%)
  Pallas kernels  27.2 us (23%)
  waiting for transfers between devices  25.8 us (22%)
  blocking collectives  20.4 us (17%)
  local copies, waits for them, and re-layouts  1.54 us (1%)
    ppermute x14, starting transfers between devices, swapped(): lax.ppermute(value, 'rows', [(i, i ^ mask) for i in range(lax.axis_size('...  31.7 us
    pallas_call x14, Pallas kernels, call(): return lambda *operands: run(*operands, *after)  27.2 us
    ppermute x4, waiting for transfers between devices, around(): lax.ppermute(value, 'rows', [(i, (i + (2 if i % 2 == 0 else -2)) % size)...  23.4 us
    all_to_all x1, blocking collectives, shards(): lax.all_to_all(jnp.broadcast_to(stats, (size,) + stats.shape), 'rows', 0, 0)  20.4 us
    ppermute x4, starting transfers between devices, around(): lax.ppermute(value, 'rows', [(i, (i + (2 if i % 2 == 0 else -2)) % size)...  9.35 us
    ppermute x2, starting transfers between devices, shifted(): lax.ppermute(value, 'rows', [(i, (i + step) % size) for i in range(size)])  2.82 us
  transfers between devices with their start and end apart: 20, of which 6 were waited for; matrix products, arithmetic and copies ran while one was open for 0% of the time, Pallas kernels for 17%

profile of v2, /device:TPU:1, one launch (start us, length us, event | category | flops | bytes accessed | tf_op | source)
XLA Modules:
  0.0 119.8 jit_solution(3722708414612364156)
XLA Ops:
  0.6 4.1 %shard_map.68 = (bf16[2,256,256]{2,1,0:T(8,128)(2,1)}, bf16[2,256,256]{2,1,0:T(8,128)(2,1)}, bf16[4,256,128]{2,1,0:T(8,128)(2,1)}, bf16[4,256,128]{2,1,0:T(8,128)(2,1)}) custom-call(s32[4,6]{1,0:T(4,128)} %bitcast.2, f32[4,4,2,128,256]{4,3,2,1,0:T(8,128)} %basis.3, bf16[6,4,4,128,128]{4,3,2,1,0:T(8,128)(2,1)} %weights.15), custom_call_target="tpu_custom_call" | custom-call | flops 1 | bytes 1 | tf_op jit(solution)/shard_map/pallas_call | solution.py:38
  4.7 3.3 %collective-permute-start = (bf16[4,256,128]{2,1,0:T(8,128)(2,1)}, bf16[4,256,128]{2,1,0:T(8,128)(2,1)S(1)}, u32[]{:S(2)}, u32[]{:S(2)}) collective-permute-start(bf16[4,256,128]{2,1,0:T(8,128)(2,1)} %get-tuple-element.26.own), channel_id=1, source_target_pairs={{0,1},{1,0},{2,3},{3,2},{4,5},{5,4},{6,7},{7,6},{8,9},{9,8},{10,11... | collective-permute-start | bytes 786440 | tf_op jit(solution)/shard_map/ppermute | solution.py:335
  8.0 0.1 collective-permute-start.3
  8.2 1.2 %collective-permute-done.far = bf16[4,256,128]{2,1,0:T(8,128)(2,1)S(1)} collective-permute-done((bf16[4,256,128]{2,1,0:T(8,128)(2,1)}, bf16[4,256,128]{2,1,0:T(8,128)(2,1)S(1)}, u32[]{:S(2)}, u32[]{:S(2)}) %collective-permute-start) | collective-permute-done | bytes 262176 | tf_op jit(solution)/shard_map/ppermute | solution.py:335
  9.4 1.5 %copy-done.7 = bf16[4,256,128]{2,1,0:T(8,128)(2,1)S(1)} copy-done((bf16[4,256,128]{2,1,0:T(8,128)(2,1)S(1)}, bf16[4,256,128]{2,1,0:T(8,128)(2,1)}, u32[]{:S(2)}) %copy-start.7) | copy-done | bytes 262168
  10.9 1.0 shard_map.69.rest_0_.own
  11.9 0.1 collective-permute-start.1
  12.0 3.0 %shard_map.70 = (bf16[4,288,128]{2,1,0:T(8,128)(2,1)S(1)}, f32[4,4,2,128,256]{4,3,2,1,0:T(8,128)S(1)}) custom-call(s32[2,32]{1,0:T(2,128)S(1)} %bitcast.11, bf16[32,2,128,128]{3,2,1,0:T(8,128)(2,1)S(1)} %copy-done.5, f32[4,4,2,128,256]{4,3,2,1,0:T(8,128)S(1)} %copy-done.1, bf16[4,256,128]{2,1,0:T(8,128)(2,1)S(1)} %shard_map.69.rest_0_.own), custom_call_target="tpu_custom_call" | custom-call | flops 20000000000 | bytes 1 | tf_op jit(solution)/shard_map/pallas_call | solution.py:38
  15.0 0.2 collective-permute-start.2
  15.2 0.0 collective-permute-done.3.far
  15.2 1.0 shard_map.71.own
  16.2 1.6 %collective-permute-start.6 = (bf16[4,256,128]{2,1,0:T(8,128)(2,1)S(1)}, bf16[4,256,128]{2,1,0:T(8,128)(2,1)S(1)}, u32[]{:S(2)}, u32[]{:S(2)}) collective-permute-start(bf16[4,256,128]{2,1,0:T(8,128)(2,1)S(1)} %shard_map.71.own), channel_id=1, source_target_pairs={{0,2},{1,3},{2,0},{3,1},{4,6},{5,7},{6,4},{7,5},{8,10},{9,11},{10,... | collective-permute-start | bytes 786440 | tf_op jit(solution)/shard_map/ppermute | solution.py:335
  17.9 0.1 pad_maximum_fusion.rest_0_
  17.9 0.0 copy-start.2
  18.0 3.9 %collective-permute-start.5 = (bf16[8,288,128]{2,1,0:T(8,128)(2,1)S(1)}, bf16[8,288,128]{2,1,0:T(8,128)(2,1)S(1)}, u32[]{:S(2)}, u32[]{:S(2)}) collective-permute-start(bf16[8,288,128]{2,1,0:T(8,128)(2,1)S(1)} %pad_maximum_fusion.rest_0_), channel_id=1, source_target_pairs={{0,2},{1,15},{2,4},{3,1},{4,6},{5,3},{6,8},{7,5},{8,10},{9,7},{10,... | collective-permute-start | bytes 1769480 | tf_op jit(solution)/shard_map/ppermute | solution.py:345
  21.9 1.0 shard_map.72.rest_0_.own
  22.9 0.1 collective-permute-start.4
  23.0 2.8 %collective-permute-start.8 = (bf16[2,256,256]{2,1,0:T(8,128)(2,1)S(1)}, bf16[2,256,256]{2,1,0:T(8,128)(2,1)S(1)}, u32[]{:S(2)}, u32[]{:S(2)}) collective-permute-start(bf16[2,256,256]{2,1,0:T(8,128)(2,1)S(1)} %copy-done.3), channel_id=1, source_target_pairs={{0,1},{1,2},{2,3},{3,4},{4,5},{5,6},{6,7},{7,8},{8,9},{9,10},{10,1... | collective-permute-start | bytes 786440 | tf_op jit(solution)/shard_map/ppermute | solution.py:340
  25.8 1.0 shard_map.73.own
  26.8 1.3 %collective-permute-start.16 = (bf16[4,256,128]{2,1,0:T(8,128)(2,1)S(1)}, bf16[4,256,128]{2,1,0:T(8,128)(2,1)S(1)}, u32[]{:S(2)}, u32[]{:S(2)}) collective-permute-start(bf16[4,256,128]{2,1,0:T(8,128)(2,1)S(1)} %shard_map.73.own), channel_id=1, source_target_pairs={{0,4},{1,5},{2,6},{3,7},{4,0},{5,1},{6,2},{7,3},{8,12},{9,13},{10,... | collective-permute-start | bytes 786440 | tf_op jit(solution)/shard_map/ppermute | solution.py:335
  28.1 13.6 %collective-permute-done.5.rest_0_.rest_2_.rest_4_.rest_5_.rest_7_ = bf16[8,288,128]{2,1,0:T(8,128)(2,1)S(1)} collective-permute-done((bf16[8,288,128]{2,1,0:T(8,128)(2,1)S(1)}, bf16[8,288,128]{2,1,0:T(8,128)(2,1)S(1)}, u32[]{:S(2)}, u32[]{:S(2)}) %collective-permute-start.5) | collective-permute-done | bytes 589856 | tf_op jit(solution)/shard_map/ppermute | solution.py:345
  41.7 0.0 collective-permute-start.7
  41.7 0.0 collective-permute-done.8.before
  41.7 0.0 collective-permute-start.10
  41.7 0.0 collective-permute-done.9.after
  41.7 3.8 %shard_map.74 = (f32[4,256,128]{2,1,0:T(8,128)S(1)}, f32[4,256,128]{2,1,0:T(8,128)S(1)}) custom-call(s32[2,32]{1,0:T(2,128)S(1)} %bitcast.12, bf16[32,2,128,128]{3,2,1,0:T(8,128)(2,1)S(1)} %copy-done.5, bf16[2,256,256]{2,1,0:T(8,128)(2,1)S(1)} %collective-permute-done.8.before, bf16[2,256,256]{2,1,0:T(8,128)(2,1)S(1)} %copy-done.2, ...), custom_call_target="tpu_custom_call" | custom-call | flops 20000000000 | bytes 1 | tf_op jit(solution)/shard_map/pallas_call | solution.py:38
  45.5 9.2 %collective-permute-done.7.rest_0_.rest_6_.rest_8_.rest_9_.rest_11_ = bf16[8,288,128]{2,1,0:T(8,128)(2,1)S(1)} collective-permute-done((bf16[8,288,128]{2,1,0:T(8,128)(2,1)S(1)}, bf16[8,288,128]{2,1,0:T(8,128)(2,1)S(1)}, u32[]{:S(2)}, u32[]{:S(2)}) %collective-permute-start.7) | collective-permute-done | bytes 589856 | tf_op jit(solution)/shard_map/ppermute | solution.py:345
  54.7 0.0 collective-permute-done.10.rest_3_.rest_5_.rest_6_.rest_8_
  54.7 0.3 collective-permute-start.12
  55.0 4.9 %collective-permute-start.13 = (bf16[8,288,128]{2,1,0:T(8,128)(2,1)S(1)}, bf16[8,288,128]{2,1,0:T(8,128)(2,1)S(1)}, u32[]{:S(2)}, u32[]{:S(2)}) collective-permute-start(bf16[8,288,128]{2,1,0:T(8,128)(2,1)S(1)} %collective-permute-done.7.rest_0_.rest_6_.rest_8_.rest_9_.rest_11_), channel_id=1, source_target_pairs={{0,1},{1,0},{2,3},{3,2},{4,5},{5,4},{6,7},{7,6},{8,9},{9,8},{10,11... | collective-permute-start | bytes 1769480 | tf_op jit(solution)/shard_map/ppermute | solution.py:335
  59.9 0.0 collective-permute-done.4.far
  59.9 1.0 shard_map.75.own
  60.9 5.0 %collective-permute-start.11 = (bf16[4,256,128]{2,1,0:T(8,128)(2,1)S(1)}, bf16[4,256,128]{2,1,0:T(8,128)(2,1)S(1)}, u32[]{:S(2)}, u32[]{:S(2)}) collective-permute-start(bf16[4,256,128]{2,1,0:T(8,128)(2,1)S(1)} %shard_map.75.own), channel_id=1, source_target_pairs={{0,8},{1,9},{2,10},{3,11},{4,12},{5,13},{6,14},{7,15},{8,0},{9,1},... | collective-permute-start | bytes 786440 | tf_op jit(solution)/shard_map/ppermute | solution.py:335
  65.9 0.6 collective-permute-done.12.rest_0_.rest_10_.rest_12_.rest_13_.rest_15_
  66.5 5.1 %collective-permute-start.14 = (bf16[4,288,128]{2,1,0:T(8,128)(2,1)S(1)}, bf16[4,288,128]{2,1,0:T(8,128)(2,1)S(1)}, u32[]{:S(2)}, u32[]{:S(2)}) collective-permute-start(bf16[4,288,128]{2,1,0:T(8,128)(2,1)S(1)} %slice.3), channel_id=1, source_target_pairs={{0,2},{1,15},{2,4},{3,1},{4,6},{5,3},{6,8},{7,5},{8,10},{9,7},{10,... | collective-permute-start | bytes 884744 | tf_op jit(solution)/shard_map/ppermute | solution.py:345
  71.7 6.7 %collective-permute-start.15 = (bf16[8,288,128]{2,1,0:T(8,128)(2,1)S(1)}, bf16[8,288,128]{2,1,0:T(8,128)(2,1)S(1)}, u32[]{:S(2)}, u32[]{:S(2)}) collective-permute-start(bf16[8,288,128]{2,1,0:T(8,128)(2,1)S(1)} %collective-permute-done.12.rest_0_.rest_10_.rest_12_.rest_13_.rest_15_), channel_id=1, source_target_pairs={{0,1},{1,0},{2,3},{3,2},{4,5},{5,4},{6,7},{7,6},{8,9},{9,8},{10,11... | collective-permute-start | bytes 1769480 | tf_op jit(solution)/shard_map/ppermute | solution.py:335
  78.3 1.0 shard_map.76.rest_16_.own
  79.3 7.8 %collective-permute-start.19 = (bf16[4,256,128]{2,1,0:T(8,128)(2,1)S(1)}, bf16[4,256,128]{2,1,0:T(8,128)(2,1)S(1)}, u32[]{:S(2)}, u32[]{:S(2)}) collective-permute-start(bf16[4,256,128]{2,1,0:T(8,128)(2,1)S(1)} %shard_map.76.rest_16_.own), channel_id=1, source_target_pairs={{0,8},{1,9},{2,10},{3,11},{4,12},{5,13},{6,14},{7,15},{8,0},{9,1},... | collective-permute-start | bytes 786440 | tf_op jit(solution)/shard_map/ppermute | solution.py:335
  87.1 4.0 %shard_map.77 = (f32[4,256,128]{2,1,0:T(8,128)S(1)}, f32[4,256,128]{2,1,0:T(8,128)S(1)}) custom-call(bf16[2,256,256]{2,1,0:T(8,128)(2,1)S(1)} %collective-permute-done.8.before, bf16[2,256,256]{2,1,0:T(8,128)(2,1)S(1)} %copy-done.2, bf16[2,256,256]{2,1,0:T(8,128)(2,1)S(1)} %copy-done.3, bf16[2,256,256]{2,1,0:T(8,128)(2,1)S(1)} %collective-permute-done.9.after, ...), custom_call_target="tpu_custom_call" | custom-call | flops 1 | bytes 1 | tf_op jit(solution)/shard_map/pallas_call | solution.py:38
  91.2 0.1 collective-permute-start.17
  91.3 0.5 collective-permute-start.18
  91.8 0.9 collective-permute-done.17.rest_1_
  92.6 0.2 collective-permute-done.18.rest_2_
  92.8 2.0 %shard_map.78 = (f32[4,256,128]{2,1,0:T(8,128)S(1)}, f32[4,256,128]{2,1,0:T(8,128)S(1)}, f32[16,256]{1,0:T(8,128)S(1)}) custom-call(bf16[2,256,256]{2,1,0:T(8,128)(2,1)S(1)} %collective-permute-done.8.before, bf16[2,256,256]{2,1,0:T(8,128)(2,1)S(1)} %copy-done.2, bf16[2,256,256]{2,1,0:T(8,128)(2,1)S(1)} %copy-done.3, ...), custom_call_target="tpu_custom_call" | custom-call | flops 1 | bytes 1 | tf_op jit(solution)/shard_map/pallas_call | solution.py:38
  94.9 1.4 %shard_map.79 = (f32[4,256,128]{2,1,0:T(8,128)S(1)}, f32[9,128]{1,0:T(8,128)S(1)}) custom-call(s32[4,6]{1,0:T(4,128)S(1)} %bitcast.9, bf16[4,256,128]{2,1,0:T(8,128)(2,1)S(1)} %shard_map.75.own, bf16[4,256,128]{2,1,0:T(8,128)(2,1)S(1)} %collective-permute-done.11.rest_19_.far, bf16[6,4,4,128,128]{4,3,2,1,0:T(8,128)(2,1)S(1)} %copy-done, ...), custom_call_target="tpu_custom_call" | custom-call | flops 1 | bytes 1 | tf_op jit(solution)/shard_map/pallas_call | solution.py:38
  96.3 1.4 %shard_map.80 = (f32[4,256,128]{2,1,0:T(8,128)S(1)}, f32[9,128]{1,0:T(8,128)S(1)}) custom-call(s32[4,6]{1,0:T(4,128)S(1)} %bitcast.10, bf16[4,256,128]{2,1,0:T(8,128)(2,1)S(1)} %shard_map.76.rest_16_.own, bf16[4,256,128]{2,1,0:T(8,128)(2,1)S(1)} %collective-permute-done.19.far, bf16[6,4,4,128,128]{4,3,2,1,0:T(8,128)(2,1)S(1)} %copy-done, ...), custom_call_target="tpu_custom_call" | custom-call | flops 1 | bytes 1 | tf_op jit(solution)/shard_map/pallas_call | solution.py:38
  97.7 20.4 %all_to_all.5.shared = f32[16,18,128]{2,1,0:T(8,128)S(1)} all-to-all(f32[16,18,128]{2,1,0:T(8,128)S(1)} %broadcast_in_dim.3), channel_id=1, replica_groups=mesh['freq'=16,'rows'=16] {'rows'}, dimensions={0} | all-to-all | bytes 294912 | tf_op jit(solution)/shard_map/all_to_all | solution.py:505
  118.1 1.7 %shard_map.81 = (f32[4,2,128,256]{3,2,1,0:T(8,128)}, f32[5,2,256]{2,1,0:T(2,128)}) custom-call(f32[16,18,128]{2,1,0:T(8,128)S(1)} %all_to_all.5.shared, f32[16,256]{1,0:T(8,128)S(1)} %get-tuple-element.47.gram, f32[4,4,2,128,256]{4,3,2,1,0:T(8,128)S(1)} %get-tuple-element.43.basis, f32[4,256,128]{2,1,0:T(8,128)S(1)} %get-tuple-element.48.rest_0_, ...), custom_call_target="tpu_custom_call" | custom-call | flops 1 | bytes 1 | tf_op jit(solution)/shard_map/pallas_call | solution.py:38
  (30 shorter events, 0.1 us)
Async XLA Ops:
  0.6 8.8 %copy-start.4 = (s32[6,4]{0,1:T(4,128)S(1)}, s32[6,4]{0,1:T(4,128)}, u32[]{:S(2)}) copy-start(s32[6,4]{0,1:T(4,128)} %param.9) | copy-start | bytes 292
  0.6 8.8 %copy-start = (bf16[6,4,4,128,128]{4,3,2,1,0:T(8,128)(2,1)S(1)}, bf16[6,4,4,128,128]{4,3,2,1,0:T(8,128)(2,1)}, u32[]{:S(2)}) copy-start(bf16[6,4,4,128,128]{4,3,2,1,0:T(8,128)(2,1)} %weights.15) | copy-start | bytes 9437188
  4.7 4.7 %collective-permute-start = (bf16[4,256,128]{2,1,0:T(8,128)(2,1)}, bf16[4,256,128]{2,1,0:T(8,128)(2,1)S(1)}, u32[]{:S(2)}, u32[]{:S(2)}) collective-permute-start(bf16[4,256,128]{2,1,0:T(8,128)(2,1)} %get-tuple-element.26.own), channel_id=1, source_target_pairs={{0,1},{1,0},{2,3},{3,2},{4,5},{5,4},{6,7},{7,6},{8,9},{9,8},{10,11... | collective-permute-start | bytes 786440 | tf_op jit(solution)/shard_map/ppermute | solution.py:335
  8.0 3.9 %copy-start.8 = (s32[32,2]{0,1:T(2,128)S(1)}, s32[32,2]{0,1:T(2,128)}, u32[]{:S(2)}) copy-start(s32[32,2]{0,1:T(2,128)} %param.7) | copy-start | bytes 772
  8.0 3.9 %copy-start.1 = (f32[4,4,2,128,256]{4,3,2,1,0:T(8,128)S(1)}, f32[4,4,2,128,256]{4,3,2,1,0:T(8,128)}, u32[]{:S(2)}) copy-start(f32[4,4,2,128,256]{4,3,2,1,0:T(8,128)} %basis.3) | copy-start | bytes 12582916
  8.0 3.9 %copy-start.5 = (bf16[32,2,128,128]{3,2,1,0:T(8,128)(2,1)S(1)}, bf16[32,2,128,128]{3,2,1,0:T(8,128)(2,1)}, u32[]{:S(2)}) copy-start(bf16[32,2,128,128]{3,2,1,0:T(8,128)(2,1)} %near_blocks.1) | copy-start | bytes 6291460
  8.0 7.2 %collective-permute-start.3 = (bf16[4,256,128]{2,1,0:T(8,128)(2,1)}, bf16[4,256,128]{2,1,0:T(8,128)(2,1)S(1)}, u32[]{:S(2)}, u32[]{:S(2)}) collective-permute-start(bf16[4,256,128]{2,1,0:T(8,128)(2,1)} %get-tuple-element.28.own), channel_id=1, source_target_pairs={{0,1},{1,0},{2,3},{3,2},{4,5},{5,4},{6,7},{7,6},{8,9},{9,8},{10,11... | collective-permute-start | bytes 786440 | tf_op jit(solution)/shard_map/ppermute | solution.py:335
  9.4 1.5 %copy-start.7 = (bf16[4,256,128]{2,1,0:T(8,128)(2,1)S(1)}, bf16[4,256,128]{2,1,0:T(8,128)(2,1)}, u32[]{:S(2)}) copy-start(bf16[4,256,128]{2,1,0:T(8,128)(2,1)} %get-tuple-element.26.own) | copy-start | bytes 786436
  11.9 10.0 %collective-permute-start.1 = (bf16[4,256,128]{2,1,0:T(8,128)(2,1)S(1)}, bf16[4,256,128]{2,1,0:T(8,128)(2,1)S(1)}, u32[]{:S(2)}, u32[]{:S(2)}) collective-permute-start(bf16[4,256,128]{2,1,0:T(8,128)(2,1)S(1)} %shard_map.69.rest_0_.own), channel_id=1, source_target_pairs={{0,2},{1,3},{2,0},{3,1},{4,6},{5,7},{6,4},{7,5},{8,10},{9,11},{10,... | collective-permute-start | bytes 786440 | tf_op jit(solution)/shard_map/ppermute | solution.py:335
  12.0 3.2 %copy-start.6 = (bf16[4,256,128]{2,1,0:T(8,128)(2,1)S(1)}, bf16[4,256,128]{2,1,0:T(8,128)(2,1)}, u32[]{:S(2)}) copy-start(bf16[4,256,128]{2,1,0:T(8,128)(2,1)} %get-tuple-element.28.own) | copy-start | bytes 786436
  15.0 2.9 %collective-permute-start.2 = (bf16[4,288,128]{2,1,0:T(8,128)(2,1)S(1)}, bf16[4,288,128]{2,1,0:T(8,128)(2,1)S(1)}, u32[]{:S(2)}, u32[]{:S(2)}) collective-permute-start(bf16[4,288,128]{2,1,0:T(8,128)(2,1)S(1)} %get-tuple-element.27.rest_0_.rest_3_), channel_id=1, source_target_pairs={{0,1},{1,0},{2,3},{3,2},{4,5},{5,4},{6,7},{7,6},{8,9},{9,8},{10,11... | collective-permute-start | bytes 884744 | tf_op jit(solution)/shard_map/ppermute | solution.py:335
  16.2 9.6 %collective-permute-start.6 = (bf16[4,256,128]{2,1,0:T(8,128)(2,1)S(1)}, bf16[4,256,128]{2,1,0:T(8,128)(2,1)S(1)}, u32[]{:S(2)}, u32[]{:S(2)}) collective-permute-start(bf16[4,256,128]{2,1,0:T(8,128)(2,1)S(1)} %shard_map.71.own), channel_id=1, source_target_pairs={{0,2},{1,3},{2,0},{3,1},{4,6},{5,7},{6,4},{7,5},{8,10},{9,11},{10,... | collective-permute-start | bytes 786440 | tf_op jit(solution)/shard_map/ppermute | solution.py:335
  17.9 5.0 %copy-start.3 = (bf16[2,256,256]{2,1,0:T(8,128)(2,1)S(1)}, bf16[2,256,256]{2,1,0:T(8,128)(2,1)}, u32[]{:S(2)}) copy-start(bf16[2,256,256]{2,1,0:T(8,128)(2,1)} %get-tuple-element.32.high) | copy-start | bytes 786436
  17.9 7.9 %copy-start.2 = (bf16[2,256,256]{2,1,0:T(8,128)(2,1)S(1)}, bf16[2,256,256]{2,1,0:T(8,128)(2,1)}, u32[]{:S(2)}) copy-start(bf16[2,256,256]{2,1,0:T(8,128)(2,1)} %get-tuple-element.34.low) | copy-start | bytes 786436
  18.0 23.7 %collective-permute-start.5 = (bf16[8,288,128]{2,1,0:T(8,128)(2,1)S(1)}, bf16[8,288,128]{2,1,0:T(8,128)(2,1)S(1)}, u32[]{:S(2)}, u32[]{:S(2)}) collective-permute-start(bf16[8,288,128]{2,1,0:T(8,128)(2,1)S(1)} %pad_maximum_fusion.rest_0_), channel_id=1, source_target_pairs={{0,2},{1,15},{2,4},{3,1},{4,6},{5,3},{6,8},{7,5},{8,10},{9,7},{10,... | collective-permute-start | bytes 1769480 | tf_op jit(solution)/shard_map/ppermute | solution.py:345
  22.9 37.0 %collective-permute-start.4 = (bf16[4,256,128]{2,1,0:T(8,128)(2,1)S(1)}, bf16[4,256,128]{2,1,0:T(8,128)(2,1)S(1)}, u32[]{:S(2)}, u32[]{:S(2)}) collective-permute-start(bf16[4,256,128]{2,1,0:T(8,128)(2,1)S(1)} %shard_map.72.rest_0_.own), channel_id=1, source_target_pairs={{0,4},{1,5},{2,6},{3,7},{4,0},{5,1},{6,2},{7,3},{8,12},{9,13},{10,... | collective-permute-start | bytes 786440 | tf_op jit(solution)/shard_map/ppermute | solution.py:335
  23.0 18.7 %collective-permute-start.8 = (bf16[2,256,256]{2,1,0:T(8,128)(2,1)S(1)}, bf16[2,256,256]{2,1,0:T(8,128)(2,1)S(1)}, u32[]{:S(2)}, u32[]{:S(2)}) collective-permute-start(bf16[2,256,256]{2,1,0:T(8,128)(2,1)S(1)} %copy-done.3), channel_id=1, source_target_pairs={{0,1},{1,2},{2,3},{3,4},{4,5},{5,6},{6,7},{7,8},{8,9},{9,10},{10,1... | collective-permute-start | bytes 786440 | tf_op jit(solution)/shard_map/ppermute | solution.py:340
  25.8 15.9 %collective-permute-start.9 = (bf16[2,256,256]{2,1,0:T(8,128)(2,1)S(1)}, bf16[2,256,256]{2,1,0:T(8,128)(2,1)S(1)}, u32[]{:S(2)}, u32[]{:S(2)}) collective-permute-start(bf16[2,256,256]{2,1,0:T(8,128)(2,1)S(1)} %copy-done.2), channel_id=1, source_target_pairs={{0,15},{1,0},{2,1},{3,2},{4,3},{5,4},{6,5},{7,6},{8,7},{9,8},{10,9... | collective-permute-start | bytes 786440 | tf_op jit(solution)/shard_map/ppermute | solution.py:340
  26.8 51.5 %collective-permute-start.16 = (bf16[4,256,128]{2,1,0:T(8,128)(2,1)S(1)}, bf16[4,256,128]{2,1,0:T(8,128)(2,1)S(1)}, u32[]{:S(2)}, u32[]{:S(2)}) collective-permute-start(bf16[4,256,128]{2,1,0:T(8,128)(2,1)S(1)} %shard_map.73.own), channel_id=1, source_target_pairs={{0,4},{1,5},{2,6},{3,7},{4,0},{5,1},{6,2},{7,3},{8,12},{9,13},{10,... | collective-permute-start | bytes 786440 | tf_op jit(solution)/shard_map/ppermute | solution.py:335
  41.7 13.0 %collective-permute-start.7 = (bf16[8,288,128]{2,1,0:T(8,128)(2,1)S(1)}, bf16[8,288,128]{2,1,0:T(8,128)(2,1)S(1)}, u32[]{:S(2)}, u32[]{:S(2)}) collective-permute-start(bf16[8,288,128]{2,1,0:T(8,128)(2,1)S(1)} %collective-permute-done.5.rest_0_.rest_2_.rest_4_.rest_5_.rest_7_), channel_id=1, source_target_pairs={{0,2},{1,15},{2,4},{3,1},{4,6},{5,3},{6,8},{7,5},{8,10},{9,7},{10,... | collective-permute-start | bytes 1769480 | tf_op jit(solution)/shard_map/ppermute | solution.py:345
  41.7 13.0 %collective-permute-start.10 = (bf16[8,288,128]{2,1,0:T(8,128)(2,1)S(1)}, bf16[8,288,128]{2,1,0:T(8,128)(2,1)S(1)}, u32[]{:S(2)}, u32[]{:S(2)}) collective-permute-start(bf16[8,288,128]{2,1,0:T(8,128)(2,1)S(1)} %collective-permute-done.5.rest_0_.rest_2_.rest_4_.rest_5_.rest_7_), channel_id=1, source_target_pairs={{0,1},{1,0},{2,3},{3,2},{4,5},{5,4},{6,7},{7,6},{8,9},{9,8},{10,11... | collective-permute-start | bytes 1769480 | tf_op jit(solution)/shard_map/ppermute | solution.py:335
  54.7 11.8 %collective-permute-start.12 = (bf16[8,288,128]{2,1,0:T(8,128)(2,1)S(1)}, bf16[8,288,128]{2,1,0:T(8,128)(2,1)S(1)}, u32[]{:S(2)}, u32[]{:S(2)}) collective-permute-start(bf16[8,288,128]{2,1,0:T(8,128)(2,1)S(1)} %collective-permute-done.7.rest_0_.rest_6_.rest_8_.rest_9_.rest_11_), channel_id=1, source_target_pairs={{0,2},{1,15},{2,4},{3,1},{4,6},{5,3},{6,8},{7,5},{8,10},{9,7},{10,... | collective-permute-start | bytes 1769480 | tf_op jit(solution)/shard_map/ppermute | solution.py:345
  55.0 11.5 %collective-permute-start.13 = (bf16[8,288,128]{2,1,0:T(8,128)(2,1)S(1)}, bf16[8,288,128]{2,1,0:T(8,128)(2,1)S(1)}, u32[]{:S(2)}, u32[]{:S(2)}) collective-permute-start(bf16[8,288,128]{2,1,0:T(8,128)(2,1)S(1)} %collective-permute-done.7.rest_0_.rest_6_.rest_8_.rest_9_.rest_11_), channel_id=1, source_target_pairs={{0,1},{1,0},{2,3},{3,2},{4,5},{5,4},{6,7},{7,6},{8,9},{9,8},{10,11... | collective-permute-start | bytes 1769480 | tf_op jit(solution)/shard_map/ppermute | solution.py:335
  60.9 30.9 %collective-permute-start.11 = (bf16[4,256,128]{2,1,0:T(8,128)(2,1)S(1)}, bf16[4,256,128]{2,1,0:T(8,128)(2,1)S(1)}, u32[]{:S(2)}, u32[]{:S(2)}) collective-permute-start(bf16[4,256,128]{2,1,0:T(8,128)(2,1)S(1)} %shard_map.75.own), channel_id=1, source_target_pairs={{0,8},{1,9},{2,10},{3,11},{4,12},{5,13},{6,14},{7,15},{8,0},{9,1},... | collective-permute-start | bytes 786440 | tf_op jit(solution)/shard_map/ppermute | solution.py:335
  66.5 24.6 %collective-permute-start.14 = (bf16[4,288,128]{2,1,0:T(8,128)(2,1)S(1)}, bf16[4,288,128]{2,1,0:T(8,128)(2,1)S(1)}, u32[]{:S(2)}, u32[]{:S(2)}) collective-permute-start(bf16[4,288,128]{2,1,0:T(8,128)(2,1)S(1)} %slice.3), channel_id=1, source_target_pairs={{0,2},{1,15},{2,4},{3,1},{4,6},{5,3},{6,8},{7,5},{8,10},{9,7},{10,... | collective-permute-start | bytes 884744 | tf_op jit(solution)/shard_map/ppermute | solution.py:345
  71.7 15.4 %collective-permute-start.15 = (bf16[8,288,128]{2,1,0:T(8,128)(2,1)S(1)}, bf16[8,288,128]{2,1,0:T(8,128)(2,1)S(1)}, u32[]{:S(2)}, u32[]{:S(2)}) collective-permute-start(bf16[8,288,128]{2,1,0:T(8,128)(2,1)S(1)} %collective-permute-done.12.rest_0_.rest_10_.rest_12_.rest_13_.rest_15_), channel_id=1, source_target_pairs={{0,1},{1,0},{2,3},{3,2},{4,5},{5,4},{6,7},{7,6},{8,9},{9,8},{10,11... | collective-permute-start | bytes 1769480 | tf_op jit(solution)/shard_map/ppermute | solution.py:335
  79.3 16.9 %collective-permute-start.19 = (bf16[4,256,128]{2,1,0:T(8,128)(2,1)S(1)}, bf16[4,256,128]{2,1,0:T(8,128)(2,1)S(1)}, u32[]{:S(2)}, u32[]{:S(2)}) collective-permute-start(bf16[4,256,128]{2,1,0:T(8,128)(2,1)S(1)} %shard_map.76.rest_16_.own), channel_id=1, source_target_pairs={{0,8},{1,9},{2,10},{3,11},{4,12},{5,13},{6,14},{7,15},{8,0},{9,1},... | collective-permute-start | bytes 786440 | tf_op jit(solution)/shard_map/ppermute | solution.py:335
  91.2 1.5 %collective-permute-start.17 = (bf16[2,288,128]{2,1,0:T(8,128)(2,1)S(1)}, bf16[2,288,128]{2,1,0:T(8,128)(2,1)S(1)}, u32[]{:S(2)}, u32[]{:S(2)}) collective-permute-start(bf16[2,288,128]{2,1,0:T(8,128)(2,1)S(1)} %get-tuple-element.51), channel_id=1, source_target_pairs={{0,1},{1,0},{2,3},{3,2},{4,5},{5,4},{6,7},{7,6},{8,9},{9,8},{10,11... | collective-permute-start | bytes 442376 | tf_op jit(solution)/shard_map/ppermute | solution.py:335
  91.3 1.6 %collective-permute-start.18 = (bf16[2,288,128]{2,1,0:T(8,128)(2,1)S(1)}, bf16[2,288,128]{2,1,0:T(8,128)(2,1)S(1)}, u32[]{:S(2)}, u32[]{:S(2)}) collective-permute-start(bf16[2,288,128]{2,1,0:T(8,128)(2,1)S(1)} %get-tuple-element.50), channel_id=1, source_target_pairs={{0,1},{1,0},{2,3},{3,2},{4,5},{5,4},{6,7},{7,6},{8,9},{9,8},{10,11... | collective-permute-start | bytes 442376 | tf_op jit(solution)/shard_map/ppermute | solution.py:335

commit v3 on v2

--- a/solution.py
+++ b/solution.py
@@ -20,8 +20,10 @@
 EXTRA = 32
 INFO = 8
 BIG = 60
+GATHER = 52
+EARLY = False
 RING, NEAR, HALO = ("ring", 0), ("near", 0), ("halo", 0)
-PLAN = [(3, 0), HALO, (3, 1), RING, NEAR, RING, (4, 0), RING, (4, 1)]
+PLAN = [(3, 0), RING, HALO, (3, 1), NEAR, RING, (4, 0), RING, (4, 1)]
 COSTLY = 2 * 10**10
 
 
@@ -55,7 +57,7 @@
 
 
 def gather_kernel(scale, pairs, blocks, source, *rest):
-    out, basis, gram, slot_sem, basis_sem = rest[-5:]
+    out, gram, basis, slot_sem, basis_sem = rest[-5:]
     count, rows, lanes = out.shape
     entries = (rows - EXTRA) // 2
     vectors, nblocks = basis.shape[0], basis.shape[1]
@@ -264,6 +266,13 @@
     lax.fori_loop(0, used, body, 0)
 
 
+def hold_kernel(source, *rest):
+    held, sem = rest[-2:]
+    copy = pltpu.make_async_copy(source, held, sem)
+    copy.start()
+    copy.wait()
+
+
 def project_kernel(level, chunk, scale, partner, own, far, weights, base, basis, *rest):
     product, stats = rest[-2:]
     vectors, blocks = basis.shape[0], basis.shape[1]
@@ -398,25 +407,36 @@
     far[0] = exchanged(local_levels + 1, 0)
 
     gram_rows = vectors * vectors
-    own_slots, held = call(
+    own_slots = call(
         functools.partial(gather_kernel, scale),
-        [shape((shipped, 2 * entries + EXTRA, entries), BF16), shape(basis.shape, F32)],
+        shape((shipped, 2 * entries + EXTRA, entries), BF16),
         [SMEM, HBM, HBM],
-        [pltpu.VMEM((gram_rows, columns), F32), dma((shipped, 2)), dma((blocks,))],
+        [
+            pltpu.VMEM((gram_rows, columns), F32),
+            pltpu.VMEM(basis.shape, F32),
+            dma((shipped, 2)),
+            dma((blocks,)),
+        ],
         after=(order,),
         cost=COSTLY,
+        limit=GATHER,
     )(pairs, near_blocks, basis)
     other_slots = swapped(own_slots, 1)
 
     order = own_slots
+
+    steps = chips // 2
+    if EARLY:
+        order = behind(jnp.concatenate([own_slots, other_slots], axis=0), order)
+        pieces, theirs = [around(order)], []
+        theirs.append(swapped(pieces[0], 1))
     for c in range(1, CHUNKS):
         order = sections[c] = level_step(local_levels, c, far[c], order)
         far[c] = exchanged(local_levels + 1, c)
-
-    steps = chips // 2
-    order = behind(jnp.concatenate([own_slots, other_slots], axis=0), order)
-    pieces, theirs = [around(order)], []
-    theirs.append(swapped(pieces[0], 1))
+    if not EARLY:
+        order = behind(jnp.concatenate([own_slots, other_slots], axis=0), order)
+        pieces, theirs = [around(order)], []
+        theirs.append(swapped(pieces[0], 1))
 
     def ring_step(order):
         piece = behind(pieces[-1], order, *theirs[:-1])
@@ -449,7 +469,10 @@
                 after=(order,),
                 cost=COSTLY,
             )(pairs, near_blocks, before, low, high, after, basis)
-            order = bases[0]
+            held = call(
+                hold_kernel, shape(basis.shape, F32), [HBM], [dma], after=(bases[0],), cost=COSTLY
+            )(basis)
+            order = held
         else:
             order = sections[c] = level_step(level, c, far[c], order)
             far[c] = exchanged(level + 1, c)

time: 120 us -> 115 us (0.958)
  starting transfers between devices: 43.9 us -> 37.1 us
  waiting for transfers between devices: 25.8 us -> 32.3 us
  blocking collectives: 20.4 us -> 15.9 us
    all_to_all x1, blocking collectives: 20.4 us -> 15.9 us  [shards(): lax.all_to_all(jnp.broadcast_to(stats, (size,) + stats.shape), 'rows', 0, 0)]
    ppermute x2, waiting for transfers between devices: 0.01 us -> 4.18 us  [shifted(): lax.ppermute(value, 'rows', [(i, (i + step) % size) for i in range(size)])]
    ppermute x14, starting transfers between devices: 31.7 us -> 28.9 us  [swapped(): lax.ppermute(value, 'rows', [(i, i ^ mask) for i in range(lax.axis_size('...]
    ppermute x2, starting transfers between devices: 2.82 us -> 0.51 us  [shifted(): lax.ppermute(value, 'rows', [(i, (i + step) % size) for i in range(size)])]
    ppermute x4, waiting for transfers between devices: 23.4 us -> 25.6 us  [around(): lax.ppermute(value, 'rows', [(i, (i + (2 if i % 2 == 0 else -2)) % size)...]
    ppermute x4, starting transfers between devices: 9.35 us -> 7.74 us  [around(): lax.ppermute(value, 'rows', [(i, (i + (2 if i % 2 == 0 else -2)) % size)...]
    pallas_call x14 -> x15, Pallas kernels: 27.2 us -> 27.4 us  [call(): return lambda *operands: run(*operands, *after)]
  transfers between devices with their start and end apart: 20 -> 20, of which waited for: 6 -> 7; matrix products, arithmetic and copies ran while one was open for 0% -> 0% of each run, Pallas kernels for 17% -> 18%
where the time goes in v3:
time: 115 us
  starting transfers between devices  37.1 us (32%)
  waiting for transfers between devices  32.3 us (28%)
  Pallas kernels  27.4 us (24%)
  blocking collectives  15.9 us (14%)
    ppermute x14, starting transfers between devices, swapped(): lax.ppermute(value, 'rows', [(i, i ^ mask) for i in range(lax.axis_size('...  28.9 us
    pallas_call x15, Pallas kernels, call(): return lambda *operands: run(*operands, *after)  27.4 us
    ppermute x4, waiting for transfers between devices, around(): lax.ppermute(value, 'rows', [(i, (i + (2 if i % 2 == 0 else -2)) % size)...  25.6 us
    all_to_all x1, blocking collectives, shards(): lax.all_to_all(jnp.broadcast_to(stats, (size,) + stats.shape), 'rows', 0, 0)  15.9 us
    ppermute x4, starting transfers between devices, around(): lax.ppermute(value, 'rows', [(i, (i + (2 if i % 2 == 0 else -2)) % size)...  7.74 us
    ppermute x2, waiting for transfers between devices, shifted(): lax.ppermute(value, 'rows', [(i, (i + step) % size) for i in range(size)])  4.18 us
    ppermute x14, waiting for transfers between devices, swapped(): lax.ppermute(value, 'rows', [(i, i ^ mask) for i in range(lax.axis_size('...  2.56 us
  transfers between devices with their start and end apart: 20, of which 7 were waited for; matrix products, arithmetic and copies ran while one was open for 0% of the time, Pallas kernels for 18%

profile of v3, /device:TPU:1, one launch (start us, length us, event | category | flops | bytes accessed | tf_op | source)
XLA Modules:
  0.0 114.6 jit_solution(9796684709108816346)
XLA Ops:
  0.6 4.1 %shard_map.68 = (bf16[2,256,256]{2,1,0:T(8,128)(2,1)}, bf16[2,256,256]{2,1,0:T(8,128)(2,1)}, bf16[4,256,128]{2,1,0:T(8,128)(2,1)}, bf16[4,256,128]{2,1,0:T(8,128)(2,1)}) custom-call(s32[4,6]{1,0:T(4,128)} %bitcast.2, f32[4,4,2,128,256]{4,3,2,1,0:T(8,128)} %source.3, bf16[6,4,4,128,128]{4,3,2,1,0:T(8,128)(2,1)} %weights.15), custom_call_target="tpu_custom_call" | custom-call | flops 1 | bytes 1 | tf_op jit(solution)/shard_map/pallas_call | solution.py:40
  4.7 3.3 %collective-permute-start = (bf16[4,256,128]{2,1,0:T(8,128)(2,1)}, bf16[4,256,128]{2,1,0:T(8,128)(2,1)S(1)}, u32[]{:S(2)}, u32[]{:S(2)}) collective-permute-start(bf16[4,256,128]{2,1,0:T(8,128)(2,1)} %get-tuple-element.24.own), channel_id=1, source_target_pairs={{0,1},{1,0},{2,3},{3,2},{4,5},{5,4},{6,7},{7,6},{8,9},{9,8},{10,11... | collective-permute-start | bytes 786440 | tf_op jit(solution)/shard_map/ppermute | solution.py:344
  8.0 0.1 collective-permute-start.3
  8.2 1.3 %collective-permute-done.far = bf16[4,256,128]{2,1,0:T(8,128)(2,1)S(1)} collective-permute-done((bf16[4,256,128]{2,1,0:T(8,128)(2,1)}, bf16[4,256,128]{2,1,0:T(8,128)(2,1)S(1)}, u32[]{:S(2)}, u32[]{:S(2)}) %collective-permute-start) | collective-permute-done | bytes 262176 | tf_op jit(solution)/shard_map/ppermute | solution.py:344
  9.4 0.9 copy-done.7
  10.4 1.0 shard_map.69.rest_0_.own
  11.4 0.1 collective-permute-start.1
  11.5 3.4 %shard_map.70.rest_0_.rest_3_ = bf16[4,288,128]{2,1,0:T(8,128)(2,1)S(1)} custom-call(s32[2,32]{1,0:T(2,128)S(1)} %bitcast.11, bf16[32,2,128,128]{3,2,1,0:T(8,128)(2,1)} %near_blocks.1, f32[4,4,2,128,256]{4,3,2,1,0:T(8,128)} %source.3, bf16[4,256,128]{2,1,0:T(8,128)(2,1)S(1)} %shard_map.69.rest_0_.own), custom_call_target="tpu_custom_call" | custom-call | flops 20000000000 | bytes 1 | tf_op jit(solution)/shard_map/pallas_call | solution.py:40
  14.9 0.6 collective-permute-start.2
  15.5 1.0 shard_map.71.own
  16.5 1.7 %collective-permute-start.9 = (bf16[4,256,128]{2,1,0:T(8,128)(2,1)S(1)}, bf16[4,256,128]{2,1,0:T(8,128)(2,1)S(1)}, u32[]{:S(2)}, u32[]{:S(2)}) collective-permute-start(bf16[4,256,128]{2,1,0:T(8,128)(2,1)S(1)} %shard_map.71.own), channel_id=1, source_target_pairs={{0,2},{1,3},{2,0},{3,1},{4,6},{5,7},{6,4},{7,5},{8,10},{9,11},{10,... | collective-permute-start | bytes 786440 | tf_op jit(solution)/shard_map/ppermute | solution.py:344
  18.1 0.0 collective-permute-done.2.rest_1_.rest_4_
  18.1 0.1 pad_maximum_fusion.rest_0_
  18.2 0.0 copy-start.2
  18.2 3.9 %collective-permute-start.5 = (bf16[8,288,128]{2,1,0:T(8,128)(2,1)S(1)}, bf16[8,288,128]{2,1,0:T(8,128)(2,1)S(1)}, u32[]{:S(2)}, u32[]{:S(2)}) collective-permute-start(bf16[8,288,128]{2,1,0:T(8,128)(2,1)S(1)} %pad_maximum_fusion.rest_0_), channel_id=1, source_target_pairs={{0,2},{1,15},{2,4},{3,1},{4,6},{5,3},{6,8},{7,5},{8,10},{9,7},{10,... | collective-permute-start | bytes 1769480 | tf_op jit(solution)/shard_map/ppermute | solution.py:354
  22.1 0.0 collective-permute-done.1.far
  22.1 1.0 shard_map.72.own
  23.1 0.1 collective-permute-start.4
  23.2 13.8 %collective-permute-done.5.rest_0_.rest_2_.rest_4_.rest_5_.rest_7_ = bf16[8,288,128]{2,1,0:T(8,128)(2,1)S(1)} collective-permute-done((bf16[8,288,128]{2,1,0:T(8,128)(2,1)S(1)}, bf16[8,288,128]{2,1,0:T(8,128)(2,1)S(1)}, u32[]{:S(2)}, u32[]{:S(2)}) %collective-permute-start.5) | collective-permute-done | bytes 589856 | tf_op jit(solution)/shard_map/ppermute | solution.py:354
  37.0 0.2 collective-permute-start.6
  37.2 0.1 collective-permute-start.7
  37.3 0.5 collective-permute-start.8
  37.8 1.0 shard_map.73.rest_0_.own
  38.7 2.1 %collective-permute-start.16 = (bf16[4,256,128]{2,1,0:T(8,128)(2,1)S(1)}, bf16[4,256,128]{2,1,0:T(8,128)(2,1)S(1)}, u32[]{:S(2)}, u32[]{:S(2)}) collective-permute-start(bf16[4,256,128]{2,1,0:T(8,128)(2,1)S(1)} %shard_map.73.rest_0_.own), channel_id=1, source_target_pairs={{0,4},{1,5},{2,6},{3,7},{4,0},{5,1},{6,2},{7,3},{8,12},{9,13},{10,... | collective-permute-start | bytes 786440 | tf_op jit(solution)/shard_map/ppermute | solution.py:344
  40.8 2.6 %collective-permute-done.7.before = bf16[2,256,256]{2,1,0:T(8,128)(2,1)S(1)} collective-permute-done((bf16[2,256,256]{2,1,0:T(8,128)(2,1)S(1)}, bf16[2,256,256]{2,1,0:T(8,128)(2,1)S(1)}, u32[]{:S(2)}, u32[]{:S(2)}) %collective-permute-start.7) | collective-permute-done | bytes 262176 | tf_op jit(solution)/shard_map/ppermute | solution.py:349
  43.4 1.2 %collective-permute-start.10 = (bf16[8,288,128]{2,1,0:T(8,128)(2,1)S(1)}, bf16[8,288,128]{2,1,0:T(8,128)(2,1)S(1)}, u32[]{:S(2)}, u32[]{:S(2)}) collective-permute-start(bf16[8,288,128]{2,1,0:T(8,128)(2,1)S(1)} %collective-permute-done.5.rest_0_.rest_2_.rest_4_.rest_5_.rest_7_), channel_id=1, source_target_pairs={{0,1},{1,0},{2,3},{3,2},{4,5},{5,4},{6,7},{7,6},{8,9},{9,8},{10,11... | collective-permute-start | bytes 1769480 | tf_op jit(solution)/shard_map/ppermute | solution.py:344
  44.6 1.6 %collective-permute-done.8.after = bf16[2,256,256]{2,1,0:T(8,128)(2,1)S(1)} collective-permute-done((bf16[2,256,256]{2,1,0:T(8,128)(2,1)S(1)}, bf16[2,256,256]{2,1,0:T(8,128)(2,1)S(1)}, u32[]{:S(2)}, u32[]{:S(2)}) %collective-permute-start.8) | collective-permute-done | bytes 262176 | tf_op jit(solution)/shard_map/ppermute | solution.py:349
  46.2 3.8 %shard_map.74 = (f32[4,256,128]{2,1,0:T(8,128)S(1)}, f32[4,256,128]{2,1,0:T(8,128)S(1)}) custom-call(s32[2,32]{1,0:T(2,128)S(1)} %bitcast.12, bf16[32,2,128,128]{3,2,1,0:T(8,128)(2,1)S(1)} %copy-done.5, bf16[2,256,256]{2,1,0:T(8,128)(2,1)S(1)} %collective-permute-done.7.before, bf16[2,256,256]{2,1,0:T(8,128)(2,1)S(1)} %copy-done.2, ...), custom_call_target="tpu_custom_call" | custom-call | flops 20000000000 | bytes 1 | tf_op jit(solution)/shard_map/pallas_call | solution.py:40
  49.9 0.3 shard_map.75.basis
  50.3 3.6 %collective-permute-start.12 = (bf16[8,288,128]{2,1,0:T(8,128)(2,1)S(1)}, bf16[8,288,128]{2,1,0:T(8,128)(2,1)S(1)}, u32[]{:S(2)}, u32[]{:S(2)}) collective-permute-start(bf16[8,288,128]{2,1,0:T(8,128)(2,1)S(1)} %collective-permute-done.6.rest_0_.rest_6_.rest_8_.rest_9_.rest_11_), channel_id=1, source_target_pairs={{0,2},{1,15},{2,4},{3,1},{4,6},{5,3},{6,8},{7,5},{8,10},{9,7},{10,... | collective-permute-start | bytes 1769480 | tf_op jit(solution)/shard_map/ppermute | solution.py:354
  53.8 3.2 %collective-permute-start.13 = (bf16[8,288,128]{2,1,0:T(8,128)(2,1)S(1)}, bf16[8,288,128]{2,1,0:T(8,128)(2,1)S(1)}, u32[]{:S(2)}, u32[]{:S(2)}) collective-permute-start(bf16[8,288,128]{2,1,0:T(8,128)(2,1)S(1)} %collective-permute-done.6.rest_0_.rest_6_.rest_8_.rest_9_.rest_11_), channel_id=1, source_target_pairs={{0,1},{1,0},{2,3},{3,2},{4,5},{5,4},{6,7},{7,6},{8,9},{9,8},{10,11... | collective-permute-start | bytes 1769480 | tf_op jit(solution)/shard_map/ppermute | solution.py:344
  57.0 1.0 shard_map.76.own
  58.0 4.7 %collective-permute-start.11 = (bf16[4,256,128]{2,1,0:T(8,128)(2,1)S(1)}, bf16[4,256,128]{2,1,0:T(8,128)(2,1)S(1)}, u32[]{:S(2)}, u32[]{:S(2)}) collective-permute-start(bf16[4,256,128]{2,1,0:T(8,128)(2,1)S(1)} %shard_map.76.own), channel_id=1, source_target_pairs={{0,8},{1,9},{2,10},{3,11},{4,12},{5,13},{6,14},{7,15},{8,0},{9,1},... | collective-permute-start | bytes 786440 | tf_op jit(solution)/shard_map/ppermute | solution.py:344
  62.7 11.8 %collective-permute-done.12.rest_0_.rest_10_.rest_12_.rest_13_.rest_15_ = bf16[8,288,128]{2,1,0:T(8,128)(2,1)S(1)} collective-permute-done((bf16[8,288,128]{2,1,0:T(8,128)(2,1)S(1)}, bf16[8,288,128]{2,1,0:T(8,128)(2,1)S(1)}, u32[]{:S(2)}, u32[]{:S(2)}) %collective-permute-start.12) | collective-permute-done | bytes 589856 | tf_op jit(solution)/shard_map/ppermute | solution.py:354
  74.5 0.1 collective-permute-start.14
  74.5 0.9 collective-permute-start.15
  75.4 1.0 shard_map.77.rest_16_.own
  76.4 4.2 %collective-permute-start.19 = (bf16[4,256,128]{2,1,0:T(8,128)(2,1)S(1)}, bf16[4,256,128]{2,1,0:T(8,128)(2,1)S(1)}, u32[]{:S(2)}, u32[]{:S(2)}) collective-permute-start(bf16[4,256,128]{2,1,0:T(8,128)(2,1)S(1)} %shard_map.77.rest_16_.own), channel_id=1, source_target_pairs={{0,8},{1,9},{2,10},{3,11},{4,12},{5,13},{6,14},{7,15},{8,0},{9,1},... | collective-permute-start | bytes 786440 | tf_op jit(solution)/shard_map/ppermute | solution.py:344
  80.7 3.5 %shard_map.78 = (f32[4,256,128]{2,1,0:T(8,128)S(1)}, f32[4,256,128]{2,1,0:T(8,128)S(1)}) custom-call(bf16[2,256,256]{2,1,0:T(8,128)(2,1)S(1)} %collective-permute-done.7.before, bf16[2,256,256]{2,1,0:T(8,128)(2,1)S(1)} %copy-done.2, bf16[2,256,256]{2,1,0:T(8,128)(2,1)S(1)} %copy-done.3, bf16[2,256,256]{2,1,0:T(8,128)(2,1)S(1)} %collective-permute-done.8.after, ...), custom_call_target="tpu_custom_call" | custom-call | flops 1 | bytes 1 | tf_op jit(solution)/shard_map/pallas_call | solution.py:40
  84.2 6.7 %collective-permute-start.17 = (bf16[2,288,128]{2,1,0:T(8,128)(2,1)S(1)}, bf16[2,288,128]{2,1,0:T(8,128)(2,1)S(1)}, u32[]{:S(2)}, u32[]{:S(2)}) collective-permute-start(bf16[2,288,128]{2,1,0:T(8,128)(2,1)S(1)} %get-tuple-element.47), channel_id=1, source_target_pairs={{0,1},{1,0},{2,3},{3,2},{4,5},{5,4},{6,7},{7,6},{8,9},{9,8},{10,11... | collective-permute-start | bytes 442376 | tf_op jit(solution)/shard_map/ppermute | solution.py:344
  90.8 0.1 collective-permute-start.18
  90.9 0.9 collective-permute-done.17.rest_1_
  91.8 0.4 collective-permute-done.18.rest_2_
  92.2 2.0 %shard_map.79 = (f32[4,256,128]{2,1,0:T(8,128)S(1)}, f32[4,256,128]{2,1,0:T(8,128)S(1)}, f32[16,256]{1,0:T(8,128)S(1)}) custom-call(bf16[2,256,256]{2,1,0:T(8,128)(2,1)S(1)} %collective-permute-done.7.before, bf16[2,256,256]{2,1,0:T(8,128)(2,1)S(1)} %copy-done.2, bf16[2,256,256]{2,1,0:T(8,128)(2,1)S(1)} %copy-done.3, ...), custom_call_target="tpu_custom_call" | custom-call | flops 1 | bytes 1 | tf_op jit(solution)/shard_map/pallas_call | solution.py:40
  94.2 1.4 %shard_map.80 = (f32[4,256,128]{2,1,0:T(8,128)S(1)}, f32[9,128]{1,0:T(8,128)S(1)}) custom-call(s32[4,6]{1,0:T(4,128)S(1)} %bitcast.9, bf16[4,256,128]{2,1,0:T(8,128)(2,1)S(1)} %shard_map.76.own, bf16[4,256,128]{2,1,0:T(8,128)(2,1)S(1)} %collective-permute-done.11.rest_19_.far, bf16[6,4,4,128,128]{4,3,2,1,0:T(8,128)(2,1)S(1)} %copy-done, ...), custom_call_target="tpu_custom_call" | custom-call | flops 1 | bytes 1 | tf_op jit(solution)/shard_map/pallas_call | solution.py:40
  95.6 1.4 %shard_map.81 = (f32[4,256,128]{2,1,0:T(8,128)S(1)}, f32[9,128]{1,0:T(8,128)S(1)}) custom-call(s32[4,6]{1,0:T(4,128)S(1)} %bitcast.10, bf16[4,256,128]{2,1,0:T(8,128)(2,1)S(1)} %shard_map.77.rest_16_.own, bf16[4,256,128]{2,1,0:T(8,128)(2,1)S(1)} %collective-permute-done.19.far, bf16[6,4,4,128,128]{4,3,2,1,0:T(8,128)(2,1)S(1)} %copy-done, ...), custom_call_target="tpu_custom_call" | custom-call | flops 1 | bytes 1 | tf_op jit(solution)/shard_map/pallas_call | solution.py:40
  97.1 15.9 %all_to_all.5.shared = f32[16,18,128]{2,1,0:T(8,128)S(1)} all-to-all(f32[16,18,128]{2,1,0:T(8,128)S(1)} %broadcast_in_dim.3), channel_id=1, replica_groups=mesh['freq'=16,'rows'=16] {'rows'}, dimensions={0} | all-to-all | bytes 294912 | tf_op jit(solution)/shard_map/all_to_all | solution.py:528
  113.0 1.7 %shard_map.82 = (f32[4,2,128,256]{3,2,1,0:T(8,128)}, f32[5,2,256]{2,1,0:T(2,128)}) custom-call(f32[16,18,128]{2,1,0:T(8,128)S(1)} %all_to_all.5.shared, f32[16,256]{1,0:T(8,128)S(1)} %get-tuple-element.43.gram, f32[4,4,2,128,256]{4,3,2,1,0:T(8,128)S(1)} %shard_map.75.basis, f32[4,256,128]{2,1,0:T(8,128)S(1)} %get-tuple-element.44.rest_0_, ...), custom_call_target="tpu_custom_call" | custom-call | flops 1 | bytes 1 | tf_op jit(solution)/shard_map/pallas_call | solution.py:40
  (31 shorter events, 0.1 us)
Async XLA Ops:
  0.6 8.8 %copy-start.4 = (s32[6,4]{0,1:T(4,128)S(1)}, s32[6,4]{0,1:T(4,128)}, u32[]{:S(2)}) copy-start(s32[6,4]{0,1:T(4,128)} %param.9) | copy-start | bytes 292
  0.6 8.8 %copy-start = (bf16[6,4,4,128,128]{4,3,2,1,0:T(8,128)(2,1)S(1)}, bf16[6,4,4,128,128]{4,3,2,1,0:T(8,128)(2,1)}, u32[]{:S(2)}) copy-start(bf16[6,4,4,128,128]{4,3,2,1,0:T(8,128)(2,1)} %weights.15) | copy-start | bytes 9437188
  4.7 4.7 %collective-permute-start = (bf16[4,256,128]{2,1,0:T(8,128)(2,1)}, bf16[4,256,128]{2,1,0:T(8,128)(2,1)S(1)}, u32[]{:S(2)}, u32[]{:S(2)}) collective-permute-start(bf16[4,256,128]{2,1,0:T(8,128)(2,1)} %get-tuple-element.24.own), channel_id=1, source_target_pairs={{0,1},{1,0},{2,3},{3,2},{4,5},{5,4},{6,7},{7,6},{8,9},{9,8},{10,11... | collective-permute-start | bytes 786440 | tf_op jit(solution)/shard_map/ppermute | solution.py:344
  8.0 3.4 %copy-start.8 = (s32[32,2]{0,1:T(2,128)S(1)}, s32[32,2]{0,1:T(2,128)}, u32[]{:S(2)}) copy-start(s32[32,2]{0,1:T(2,128)} %param.7) | copy-start | bytes 772
  8.0 7.4 %collective-permute-start.3 = (bf16[4,256,128]{2,1,0:T(8,128)(2,1)}, bf16[4,256,128]{2,1,0:T(8,128)(2,1)S(1)}, u32[]{:S(2)}, u32[]{:S(2)}) collective-permute-start(bf16[4,256,128]{2,1,0:T(8,128)(2,1)} %get-tuple-element.25.own), channel_id=1, source_target_pairs={{0,1},{1,0},{2,3},{3,2},{4,5},{5,4},{6,7},{7,6},{8,9},{9,8},{10,11... | collective-permute-start | bytes 786440 | tf_op jit(solution)/shard_map/ppermute | solution.py:344
  9.4 1.0 copy-start.7
  11.4 10.8 %collective-permute-start.1 = (bf16[4,256,128]{2,1,0:T(8,128)(2,1)S(1)}, bf16[4,256,128]{2,1,0:T(8,128)(2,1)S(1)}, u32[]{:S(2)}, u32[]{:S(2)}) collective-permute-start(bf16[4,256,128]{2,1,0:T(8,128)(2,1)S(1)} %shard_map.69.rest_0_.own), channel_id=1, source_target_pairs={{0,2},{1,3},{2,0},{3,1},{4,6},{5,7},{6,4},{7,5},{8,10},{9,11},{10,... | collective-permute-start | bytes 786440 | tf_op jit(solution)/shard_map/ppermute | solution.py:344
  11.5 4.0 %copy-start.6 = (bf16[4,256,128]{2,1,0:T(8,128)(2,1)S(1)}, bf16[4,256,128]{2,1,0:T(8,128)(2,1)}, u32[]{:S(2)}) copy-start(bf16[4,256,128]{2,1,0:T(8,128)(2,1)} %get-tuple-element.25.own) | copy-start | bytes 786436
  14.9 3.3 %collective-permute-start.2 = (bf16[4,288,128]{2,1,0:T(8,128)(2,1)S(1)}, bf16[4,288,128]{2,1,0:T(8,128)(2,1)S(1)}, u32[]{:S(2)}, u32[]{:S(2)}) collective-permute-start(bf16[4,288,128]{2,1,0:T(8,128)(2,1)S(1)} %shard_map.70.rest_0_.rest_3_), channel_id=1, source_target_pairs={{0,1},{1,0},{2,3},{3,2},{4,5},{5,4},{6,7},{7,6},{8,9},{9,8},{10,11... | collective-permute-start | bytes 884744 | tf_op jit(solution)/shard_map/ppermute | solution.py:344
  16.5 21.3 %collective-permute-start.9 = (bf16[4,256,128]{2,1,0:T(8,128)(2,1)S(1)}, bf16[4,256,128]{2,1,0:T(8,128)(2,1)S(1)}, u32[]{:S(2)}, u32[]{:S(2)}) collective-permute-start(bf16[4,256,128]{2,1,0:T(8,128)(2,1)S(1)} %shard_map.71.own), channel_id=1, source_target_pairs={{0,2},{1,3},{2,0},{3,1},{4,6},{5,7},{6,4},{7,5},{8,10},{9,11},{10,... | collective-permute-start | bytes 786440 | tf_op jit(solution)/shard_map/ppermute | solution.py:344
  18.2 19.0 %copy-start.3 = (bf16[2,256,256]{2,1,0:T(8,128)(2,1)S(1)}, bf16[2,256,256]{2,1,0:T(8,128)(2,1)}, u32[]{:S(2)}) copy-start(bf16[2,256,256]{2,1,0:T(8,128)(2,1)} %get-tuple-element.29.high) | copy-start | bytes 786436
  18.2 19.1 %copy-start.2 = (bf16[2,256,256]{2,1,0:T(8,128)(2,1)S(1)}, bf16[2,256,256]{2,1,0:T(8,128)(2,1)}, u32[]{:S(2)}) copy-start(bf16[2,256,256]{2,1,0:T(8,128)(2,1)} %get-tuple-element.31.low) | copy-start | bytes 786436
  18.2 18.8 %collective-permute-start.5 = (bf16[8,288,128]{2,1,0:T(8,128)(2,1)S(1)}, bf16[8,288,128]{2,1,0:T(8,128)(2,1)S(1)}, u32[]{:S(2)}, u32[]{:S(2)}) collective-permute-start(bf16[8,288,128]{2,1,0:T(8,128)(2,1)S(1)} %pad_maximum_fusion.rest_0_), channel_id=1, source_target_pairs={{0,2},{1,15},{2,4},{3,1},{4,6},{5,3},{6,8},{7,5},{8,10},{9,7},{10,... | collective-permute-start | bytes 1769480 | tf_op jit(solution)/shard_map/ppermute | solution.py:354
  23.1 33.9 %collective-permute-start.4 = (bf16[4,256,128]{2,1,0:T(8,128)(2,1)S(1)}, bf16[4,256,128]{2,1,0:T(8,128)(2,1)S(1)}, u32[]{:S(2)}, u32[]{:S(2)}) collective-permute-start(bf16[4,256,128]{2,1,0:T(8,128)(2,1)S(1)} %shard_map.72.own), channel_id=1, source_target_pairs={{0,4},{1,5},{2,6},{3,7},{4,0},{5,1},{6,2},{7,3},{8,12},{9,13},{10,... | collective-permute-start | bytes 786440 | tf_op jit(solution)/shard_map/ppermute | solution.py:344
  37.0 13.2 %collective-permute-start.6 = (bf16[8,288,128]{2,1,0:T(8,128)(2,1)S(1)}, bf16[8,288,128]{2,1,0:T(8,128)(2,1)S(1)}, u32[]{:S(2)}, u32[]{:S(2)}) collective-permute-start(bf16[8,288,128]{2,1,0:T(8,128)(2,1)S(1)} %collective-permute-done.5.rest_0_.rest_2_.rest_4_.rest_5_.rest_7_), channel_id=1, source_target_pairs={{0,2},{1,15},{2,4},{3,1},{4,6},{5,3},{6,8},{7,5},{8,10},{9,7},{10,... | collective-permute-start | bytes 1769480 | tf_op jit(solution)/shard_map/ppermute | solution.py:354
  37.2 6.2 %collective-permute-start.7 = (bf16[2,256,256]{2,1,0:T(8,128)(2,1)S(1)}, bf16[2,256,256]{2,1,0:T(8,128)(2,1)S(1)}, u32[]{:S(2)}, u32[]{:S(2)}) collective-permute-start(bf16[2,256,256]{2,1,0:T(8,128)(2,1)S(1)} %copy-done.3), channel_id=1, source_target_pairs={{0,1},{1,2},{2,3},{3,4},{4,5},{5,6},{6,7},{7,8},{8,9},{9,10},{10,1... | collective-permute-start | bytes 786440 | tf_op jit(solution)/shard_map/ppermute | solution.py:349
  37.3 8.9 %copy-start.1 = (f32[4,4,2,128,256]{4,3,2,1,0:T(8,128)S(1)}, f32[4,4,2,128,256]{4,3,2,1,0:T(8,128)}, u32[]{:S(2)}) copy-start(f32[4,4,2,128,256]{4,3,2,1,0:T(8,128)} %source.3) | copy-start | bytes 12582916
  37.3 8.9 %copy-start.5 = (bf16[32,2,128,128]{3,2,1,0:T(8,128)(2,1)S(1)}, bf16[32,2,128,128]{3,2,1,0:T(8,128)(2,1)}, u32[]{:S(2)}) copy-start(bf16[32,2,128,128]{3,2,1,0:T(8,128)(2,1)} %near_blocks.1) | copy-start | bytes 6291460
  37.3 8.9 %collective-permute-start.8 = (bf16[2,256,256]{2,1,0:T(8,128)(2,1)S(1)}, bf16[2,256,256]{2,1,0:T(8,128)(2,1)S(1)}, u32[]{:S(2)}, u32[]{:S(2)}) collective-permute-start(bf16[2,256,256]{2,1,0:T(8,128)(2,1)S(1)} %copy-done.2), channel_id=1, source_target_pairs={{0,15},{1,0},{2,1},{3,2},{4,3},{5,4},{6,5},{7,6},{8,7},{9,8},{10,9... | collective-permute-start | bytes 786440 | tf_op jit(solution)/shard_map/ppermute | solution.py:349
  38.7 36.7 %collective-permute-start.16 = (bf16[4,256,128]{2,1,0:T(8,128)(2,1)S(1)}, bf16[4,256,128]{2,1,0:T(8,128)(2,1)S(1)}, u32[]{:S(2)}, u32[]{:S(2)}) collective-permute-start(bf16[4,256,128]{2,1,0:T(8,128)(2,1)S(1)} %shard_map.73.rest_0_.own), channel_id=1, source_target_pairs={{0,4},{1,5},{2,6},{3,7},{4,0},{5,1},{6,2},{7,3},{8,12},{9,13},{10,... | collective-permute-start | bytes 786440 | tf_op jit(solution)/shard_map/ppermute | solution.py:344
  43.4 6.9 %collective-permute-start.10 = (bf16[8,288,128]{2,1,0:T(8,128)(2,1)S(1)}, bf16[8,288,128]{2,1,0:T(8,128)(2,1)S(1)}, u32[]{:S(2)}, u32[]{:S(2)}) collective-permute-start(bf16[8,288,128]{2,1,0:T(8,128)(2,1)S(1)} %collective-permute-done.5.rest_0_.rest_2_.rest_4_.rest_5_.rest_7_), channel_id=1, source_target_pairs={{0,1},{1,0},{2,3},{3,2},{4,5},{5,4},{6,7},{7,6},{8,9},{9,8},{10,11... | collective-permute-start | bytes 1769480 | tf_op jit(solution)/shard_map/ppermute | solution.py:344
  50.3 24.2 %collective-permute-start.12 = (bf16[8,288,128]{2,1,0:T(8,128)(2,1)S(1)}, bf16[8,288,128]{2,1,0:T(8,128)(2,1)S(1)}, u32[]{:S(2)}, u32[]{:S(2)}) collective-permute-start(bf16[8,288,128]{2,1,0:T(8,128)(2,1)S(1)} %collective-permute-done.6.rest_0_.rest_6_.rest_8_.rest_9_.rest_11_), channel_id=1, source_target_pairs={{0,2},{1,15},{2,4},{3,1},{4,6},{5,3},{6,8},{7,5},{8,10},{9,7},{10,... | collective-permute-start | bytes 1769480 | tf_op jit(solution)/shard_map/ppermute | solution.py:354
  53.8 20.6 %collective-permute-start.13 = (bf16[8,288,128]{2,1,0:T(8,128)(2,1)S(1)}, bf16[8,288,128]{2,1,0:T(8,128)(2,1)S(1)}, u32[]{:S(2)}, u32[]{:S(2)}) collective-permute-start(bf16[8,288,128]{2,1,0:T(8,128)(2,1)S(1)} %collective-permute-done.6.rest_0_.rest_6_.rest_8_.rest_9_.rest_11_), channel_id=1, source_target_pairs={{0,1},{1,0},{2,3},{3,2},{4,5},{5,4},{6,7},{7,6},{8,9},{9,8},{10,11... | collective-permute-start | bytes 1769480 | tf_op jit(solution)/shard_map/ppermute | solution.py:344
  58.0 32.9 %collective-permute-start.11 = (bf16[4,256,128]{2,1,0:T(8,128)(2,1)S(1)}, bf16[4,256,128]{2,1,0:T(8,128)(2,1)S(1)}, u32[]{:S(2)}, u32[]{:S(2)}) collective-permute-start(bf16[4,256,128]{2,1,0:T(8,128)(2,1)S(1)} %shard_map.76.own), channel_id=1, source_target_pairs={{0,8},{1,9},{2,10},{3,11},{4,12},{5,13},{6,14},{7,15},{8,0},{9,1},... | collective-permute-start | bytes 786440 | tf_op jit(solution)/shard_map/ppermute | solution.py:344
  74.5 9.7 %collective-permute-start.14 = (bf16[4,288,128]{2,1,0:T(8,128)(2,1)S(1)}, bf16[4,288,128]{2,1,0:T(8,128)(2,1)S(1)}, u32[]{:S(2)}, u32[]{:S(2)}) collective-permute-start(bf16[4,288,128]{2,1,0:T(8,128)(2,1)S(1)} %slice.3), channel_id=1, source_target_pairs={{0,2},{1,15},{2,4},{3,1},{4,6},{5,3},{6,8},{7,5},{8,10},{9,7},{10,... | collective-permute-start | bytes 884744 | tf_op jit(solution)/shard_map/ppermute | solution.py:354
  74.5 6.1 %collective-permute-start.15 = (bf16[8,288,128]{2,1,0:T(8,128)(2,1)S(1)}, bf16[8,288,128]{2,1,0:T(8,128)(2,1)S(1)}, u32[]{:S(2)}, u32[]{:S(2)}) collective-permute-start(bf16[8,288,128]{2,1,0:T(8,128)(2,1)S(1)} %collective-permute-done.12.rest_0_.rest_10_.rest_12_.rest_13_.rest_15_), channel_id=1, source_target_pairs={{0,1},{1,0},{2,3},{3,2},{4,5},{5,4},{6,7},{7,6},{8,9},{9,8},{10,11... | collective-permute-start | bytes 1769480 | tf_op jit(solution)/shard_map/ppermute | solution.py:344
  76.4 19.2 %collective-permute-start.19 = (bf16[4,256,128]{2,1,0:T(8,128)(2,1)S(1)}, bf16[4,256,128]{2,1,0:T(8,128)(2,1)S(1)}, u32[]{:S(2)}, u32[]{:S(2)}) collective-permute-start(bf16[4,256,128]{2,1,0:T(8,128)(2,1)S(1)} %shard_map.77.rest_16_.own), channel_id=1, source_target_pairs={{0,8},{1,9},{2,10},{3,11},{4,12},{5,13},{6,14},{7,15},{8,0},{9,1},... | collective-permute-start | bytes 786440 | tf_op jit(solution)/shard_map/ppermute | solution.py:344
  84.2 7.7 %collective-permute-start.17 = (bf16[2,288,128]{2,1,0:T(8,128)(2,1)S(1)}, bf16[2,288,128]{2,1,0:T(8,128)(2,1)S(1)}, u32[]{:S(2)}, u32[]{:S(2)}) collective-permute-start(bf16[2,288,128]{2,1,0:T(8,128)(2,1)S(1)} %get-tuple-element.47), channel_id=1, source_target_pairs={{0,1},{1,0},{2,3},{3,2},{4,5},{5,4},{6,7},{7,6},{8,9},{9,8},{10,11... | collective-permute-start | bytes 442376 | tf_op jit(solution)/shard_map/ppermute | solution.py:344
  90.8 1.4 %collective-permute-start.18 = (bf16[2,288,128]{2,1,0:T(8,128)(2,1)S(1)}, bf16[2,288,128]{2,1,0:T(8,128)(2,1)S(1)}, u32[]{:S(2)}, u32[]{:S(2)}) collective-permute-start(bf16[2,288,128]{2,1,0:T(8,128)(2,1)S(1)} %get-tuple-element.46), channel_id=1, source_target_pairs={{0,1},{1,0},{2,3},{3,2},{4,5},{5,4},{6,7},{7,6},{8,9},{9,8},{10,11... | collective-permute-start | bytes 442376 | tf_op jit(solution)/shard_map/ppermute | solution.py:344
